TPU v7x, 128 devices: a whole 4x4x4 slice. The times are simulated.
128 devices in a mesh: tile: 8 (over y, x_hi), atom: 16 (over x_lo, z, core).
Axes of the slice: x: 4 (x_hi: 2, x_lo: 2; x = x_hi * 2 + x_lo), y: 4, z: 4, core: 2. Of those that a mesh axis runs over, the one named last changes fastest.
Arguments:
- image: bfloat16 [64, 64, 512], P(None, 'tile'), may hold values from -10 to 10
- coeffs: bfloat16 [512, 64, 512], P('atom', 'tile'), may hold values from -5 to 5
- dictionary: bfloat16 [512, 5184], P('atom'), may hold values from -0.078125 to 0.078125
- shrink: float32 [512], P('atom'), may hold values from 0.05 to 0.5
- seam_map: int32 [8, 512], replicated, may hold values from 0 to 1
Outputs:
- new_coeffs: bfloat16 [512, 64, 512], P('atom', 'tile')
- residual: bfloat16 [64, 64, 512], P(None, 'tile')
- atom_step: float32 [512, 5184], P('atom', 'tile')
All inputs are finite; a program needn't handle non-finite values.
Results may differ from a plain program's by a relative error of at most 0.0029.
Values may be sent and summed in bfloat16 or wider, within the bound.
No kernel may reach another device: no remote copies, remote signals or barrier semaphores. Data moves between devices by JAX's collectives and lax.ppermute only.
A program may use at most 64 MiB of HBM per device.

v0:
```python
import functools

import jax
import jax.numpy as jnp
from jax import lax
from jax.experimental import pallas as pl
from jax.experimental.pallas import tpu as pltpu
from jax.sharding import PartitionSpec as P

C = 64
TAP = 9
TILE_W = 512
HALO = TAP // 2
PADW = TILE_W + 256
LEFT = 128 - HALO

step_size = 0.1
eps_sq = 0.01


def rows_of(r, rows):
    return max(0, r - (TAP - 1)), min(rows - 1, r)


def shifted(row, j):
    n = row.shape[0]
    zero = jnp.zeros((n, 128), row.dtype)
    wide = jnp.concatenate([zero, row, zero], axis=1)
    return wide[:, LEFT + j : LEFT + j + TILE_W]


def synthesis_kernel(up_ref, own_ref, down_ref, wup_ref, wdown_ref, a_ref, out_ref, cols, acc):
    rows = own_ref.shape[0]
    atoms = own_ref.shape[1]
    acc[...] = jnp.zeros_like(acc)
    for r in range(rows + TAP - 1):
        if r < HALO:
            row = up_ref[r] * wup_ref[...]
        elif r < HALO + rows:
            row = own_ref[r - HALO]
        else:
            row = down_ref[r - HALO - rows] * wdown_ref[...]
        slot = r % 2
        for dx in range(TAP):
            cols[slot, dx * atoms : (dx + 1) * atoms, :] = shifted(row, dx)
        first, last = rows_of(r, rows)
        low, high = r - last, r - first
        part = jnp.dot(
            a_ref[low * C : (high + 1) * C, :], cols[slot], preferred_element_type=jnp.float32
        )
        base = (rows - 1 - last) * C
        acc[base : base + (high - low + 1) * C, :] += part
    for y in range(rows):
        out_ref[y] = acc[(rows - 1 - y) * C : (rows - y) * C, :].astype(out_ref.dtype)


def update_kernel(
    up_ref, own_ref, down_ref, wup_ref, wdown_ref, coef_ref, a_ref, shrink_ref,
    new_ref, term_ref, cols, acc, grad, scale,
):
    rows = own_ref.shape[0]
    atoms = coef_ref.shape[1]
    acc[...] = jnp.zeros_like(acc)
    grad[...] = jnp.zeros_like(grad)
    for r in range(rows + TAP - 1):
        if r < HALO:
            row = up_ref[r] * wup_ref[...]
        elif r < HALO + rows:
            row = own_ref[r - HALO]
        else:
            row = down_ref[r - HALO - rows] * wdown_ref[...]
        slot = r % 2
        for dx in range(TAP):
            cols[slot, dx * C : (dx + 1) * C, :] = shifted(row, TAP - 1 - dx)
        first, last = rows_of(r, rows)
        low, high = first + TAP - 1 - r, last + TAP - 1 - r
        acc[first * atoms : (last + 1) * atoms, :] += jnp.dot(
            a_ref[low * atoms : (high + 1) * atoms, :], cols[slot], preferred_element_type=jnp.float32
        )
        count = last - first + 1
        grad[low * atoms : (high + 1) * atoms, :] += lax.dot_general(
            coef_ref[first : last + 1].reshape(count * atoms, TILE_W),
            cols[slot],
            (((1,), (1,)), ((), ())),
            preferred_element_type=jnp.float32,
        )
    for y in range(rows):
        u = coef_ref[y].astype(jnp.float32) + step_size * acc[y * atoms : (y + 1) * atoms, :]
        new_ref[y] = (u - shrink_ref[...] * u / jnp.sqrt(u * u + eps_sq)).astype(new_ref.dtype)
    turned = jnp.transpose(grad[...]) * scale
    parts = term_ref.shape[0]
    per = C // parts
    for dx in range(TAP):
        for t in range(parts):
            term_ref[t, dx] = turned[dx * C + t * per : dx * C + (t + 1) * per, :]


def whole(count):
    return [pl.BlockSpec(memory_space=pltpu.VMEM)] * count


def per_device(image, coeffs, dictionary, shrink, seam_map):
    atoms = coeffs.shape[0]
    rows = image.shape[1]
    strips = lax.axis_size("tile")
    groups = lax.axis_size("atom")
    position = lax.axis_index("tile")
    member = lax.axis_index("atom") // 2
    seam_float = seam_map.astype(jnp.float32)
    w_down = (0.5 + 0.5 * seam_float[position]).astype(jnp.bfloat16)[None, :]
    w_up = (0.5 + 0.5 * seam_float[(position + strips - 1) % strips]).astype(jnp.bfloat16)[None, :]
    forward = [(i, (i + 1) % strips) for i in range(strips)]
    backward = [(i, (i + strips - 1) % strips) for i in range(strips)]
    chips = [[i for i in range(groups) if i % 2 == core] for core in range(2)]
    swap = [(i, i ^ 1) for i in range(groups)]

    def halos(field):
        up = lax.ppermute(field[rows - HALO :], "tile", forward)
        down = lax.ppermute(field[:HALO], "tile", backward)
        return up, down

    def exchange(field):
        return lax.all_to_all(field, "atom", 0, 0, tiled=True, axis_index_groups=chips)

    coef_rows = coeffs.transpose(1, 0, 2)
    kernel = dictionary.reshape(atoms, C, TAP, TAP)
    a_synth = kernel.transpose(2, 1, 3, 0).reshape(TAP * C, TAP * atoms)
    a_corr = kernel.transpose(2, 0, 3, 1).reshape(TAP * atoms, TAP * C)
    coef_up, coef_down = halos(coef_rows)
    params = pltpu.CompilerParams(vmem_limit_bytes=48 * 1024 * 1024)
    partial = pl.pallas_call(
        synthesis_kernel,
        out_shape=jax.ShapeDtypeStruct((rows, C, TILE_W), jnp.float32),
        in_specs=whole(6),
        out_specs=pl.BlockSpec(memory_space=pltpu.VMEM),
        scratch_shapes=[
            pltpu.VMEM((2, TAP * atoms, TILE_W), jnp.bfloat16),
            pltpu.VMEM((rows * C, TILE_W), jnp.float32),
        ],
        compiler_params=params,
    )(coef_up, coef_rows, coef_down, w_up, w_down, a_synth)
    pieces = exchange(partial.astype(jnp.float16))
    mine = jnp.sum(pieces.astype(jnp.float32), axis=0)
    mine = mine + lax.ppermute(mine, "atom", swap)
    image_row = lax.dynamic_index_in_dim(image, member, 1, keepdims=False)
    resid_row = (image_row.astype(jnp.float32) - mine).astype(jnp.bfloat16)
    resid_rows = exchange(jnp.broadcast_to(resid_row[None], (rows, C, TILE_W)))
    resid_up, resid_down = halos(resid_rows)
    residual = resid_rows.transpose(1, 0, 2)
    scale = float((rows * strips * TILE_W) ** -0.5)
    per = C // strips
    new_rows, terms = pl.pallas_call(
        functools.partial(update_kernel, scale=scale),
        out_shape=(
            jax.ShapeDtypeStruct((rows, atoms, TILE_W), jnp.bfloat16),
            jax.ShapeDtypeStruct((strips, TAP, per, TAP * atoms), jnp.float32),
        ),
        in_specs=whole(8),
        out_specs=(pl.BlockSpec(memory_space=pltpu.VMEM),) * 2,
        scratch_shapes=[
            pltpu.VMEM((2, TAP * C, TILE_W), jnp.bfloat16),
            pltpu.VMEM((rows * atoms, TILE_W), jnp.float32),
            pltpu.VMEM((TAP * atoms, TAP * C), jnp.float32),
        ],
        compiler_params=params,
    )(resid_up, resid_rows, resid_down, w_up, w_down, coef_rows, a_corr, shrink[:, None])
    new_coeffs = new_rows.transpose(1, 0, 2)
    got = lax.all_to_all(terms, "tile", 0, 0, tiled=True)
    step = jnp.sum(got, axis=0).reshape(TAP, per, TAP, atoms)
    atom_step = step.transpose(3, 1, 2, 0).reshape(atoms, per * TAP * TAP)
    return (new_coeffs, residual, atom_step)


def solution(mesh):
    placed = (P(None, "tile", None), P("atom", "tile", None), P("atom", None), P("atom"), P())
    return jax.shard_map(
        per_device,
        mesh=mesh,
        in_specs=placed,
        out_specs=(P("atom", "tile", None), P(None, "tile", None), P("atom", "tile")),
        check_vma=False,
    )
```

profile of v0, /device:TPU:0, one launch (start us, length us, event | category | flops | bytes accessed | tf_op | source)
XLA Modules:
  0.0 97.4 jit_solution(16335667714639417425)
XLA Ops:
  0.6 0.0 copy-start
  0.6 0.0 copy-start.2
  0.7 1.1 %copy.30 = bf16[32,8,512]{2,0,1:T(8,128)(2,1)S(1)} copy(bf16[32,8,512]{2,1,0:T(8,128)(2,1)} %param.6) | data formatting | bytes 524288 | tf_op args[1]
  1.8 0.7 fusion.2
  2.4 3.1 %collective-permute-start = (bf16[4,32,512]{2,1,0:T(8,128)(2,1)}, bf16[4,32,512]{2,1,0:T(8,128)(2,1)S(1)}, u32[]{:S(2)}, u32[]{:S(2)}) collective-permute-start(bf16[4,32,512]{2,1,0:T(8,128)(2,1)} %get-tuple-element.16), channel_id=1, source_target_pairs={{0,16},{16,32},{32,48},{48,64},{64,80},{80,96},{96,112},{112,0},{1... | collective-permute-start | bytes 393224 | tf_op jit(solution)/shard_map/ppermute | solution.py:118
  5.5 2.5 %collective-permute-start.1 = (bf16[4,32,512]{2,1,0:T(8,128)(2,1)S(1)}, bf16[4,32,512]{2,1,0:T(8,128)(2,1)S(1)}, u32[]{:S(2)}, u32[]{:S(2)}) collective-permute-start(bf16[4,32,512]{2,1,0:T(8,128)(2,1)S(1)} %get-tuple-element.15), channel_id=1, source_target_pairs={{0,112},{16,0},{32,16},{48,32},{64,48},{80,64},{96,80},{112,96},{1... | collective-permute-start | bytes 393224 | tf_op jit(solution)/shard_map/ppermute | solution.py:119
  8.1 1.3 %convert_element_type.28 = f32[8,512]{1,0:T(8,128)} convert(s32[8,512]{1,0:T(8,128)} %param.9) | non-fusion elementwise | flops 4096 | bytes 32768 | tf_op jit(solution)/shard_map/convert_element_type | solution.py:109
  9.4 0.0 copy-done.2
  9.4 1.6 %copy.16 = bf16[32,5184]{0,1:T(8,128)(2,1)} copy(bf16[32,5184]{1,0:T(8,128)(2,1)S(1)} %copy-done.2) | data formatting | bytes 663552 | tf_op args[2]
  11.0 2.6 %reshape.24 = bf16[32,64,9,9]{0,3,2,1:T(8,128)(2,1)S(1)} reshape(bf16[32,5184]{0,1:T(8,128)(2,1)} %copy.16) | data formatting | bytes 663552 | tf_op jit(solution)/shard_map/reshape | solution.py:126
  13.5 0.0 copy-start.1
  13.6 5.9 %copy.17 = bf16[9,64,9,32]{1,0,3,2:T(8,128)(2,1)} copy(bf16[9,64,9,32]{3,2,0,1:T(8,128)(2,1)S(1)} %bitcast.25) | data formatting | bytes 663552 | tf_op jit(solution)/shard_map/transpose | solution.py:127
  19.5 0.0 copy-done.1
  19.5 2.5 %reshape.25 = bf16[576,288]{0,1:T(8,128)(2,1)} reshape(bf16[9,64,9,32]{1,0,3,2:T(8,128)(2,1)} %copy.17) | data formatting | bytes 663552 | tf_op jit(solution)/shard_map/reshape | solution.py:127
  22.0 1.2 %copy.18.a_ref = bf16[576,288]{1,0:T(8,128)(2,1)S(1)} copy(bf16[576,288]{0,1:T(8,128)(2,1)} %reshape.25) | data formatting | bytes 663552 | tf_op jit(solution)/shard_map/reshape | solution.py:127
  23.2 0.8 add_convert_fusion
  24.0 0.0 collective-permute-done.up_ref
  24.0 0.0 collective-permute-done.1.down_ref
  24.1 2.9 %shard_map.76 = f32[8,64,512]{2,1,0:T(8,128)S(1)} custom-call(bf16[4,32,512]{2,1,0:T(8,128)(2,1)S(1)} %collective-permute-done.up_ref, bf16[8,32,512]{2,1,0:T(8,128)(2,1)S(1)} %bitcast.22, bf16[4,32,512]{2,1,0:T(8,128)(2,1)S(1)} %collective-permute-done.1.down_ref, bf16[1,512]{1,0:T(2,128)(2,1)S(1)} %get-tuple-element.18.wup_ref, ...), custom_call_target="tpu_custom_call" | custom-call | tf_op jit(solution)/shard_map/pallas_call | solution.py:131
  26.9 0.1 convert_element_type.31
  27.0 15.6 %all_to_all.15 = f16[8,64,512]{2,1,0:T(8,128)(2,1)S(1)} all-to-all(f16[8,64,512]{2,1,0:T(8,128)(2,1)S(1)} %convert_element_type.31), channel_id=1, replica_groups={{0,2,4,6,8,10,12,14},{1,3,5,7,9,11,13,15},{16,18,20,22,24,26,28,30},{17..., dimensions={0} | all-to-all | bytes 1048576 | tf_op jit(solution)/shard_map/all_to_all | solution.py:123
  42.6 0.1 convert_reduce_fusion
  42.7 0.1 collective-permute-start.2
  42.8 0.0 copy-done
  42.8 0.1 constant_dynamic-slice_fusion
  43.0 1.2 %collective-permute-done.2 = f32[64,512]{1,0:T(8,128)S(1)} collective-permute-done((f32[64,512]{1,0:T(8,128)S(1)}, f32[64,512]{1,0:T(8,128)S(1)}, u32[]{:S(2)}, u32[]{:S(2)}) %collective-permute-start.2) | collective-permute-done | bytes 131104 | tf_op jit(solution)/shard_map/ppermute | solution.py:144
  44.2 13.0 %all_to_all.16.own_ref = bf16[8,64,512]{2,1,0:T(8,128)(2,1)S(1)} all-to-all(bf16[8,64,512]{2,1,0:T(8,128)(2,1)S(1)} %broadcast_in_dim.4), channel_id=1, replica_groups={{0,2,4,6,8,10,12,14},{1,3,5,7,9,11,13,15},{16,18,20,22,24,26,28,30},{17..., dimensions={0} | all-to-all | bytes 1048576 | tf_op jit(solution)/shard_map/all_to_all | solution.py:123
  57.3 0.7 collective-permute-start.3
  58.0 5.0 %collective-permute-start.4 = (bf16[4,64,512]{2,1,0:T(8,128)(2,1)S(1)}, bf16[4,64,512]{2,1,0:T(8,128)(2,1)S(1)}, u32[]{:S(2)}, u32[]{:S(2)}) collective-permute-start(bf16[4,64,512]{2,1,0:T(8,128)(2,1)S(1)} %get-tuple-element.13), channel_id=1, source_target_pairs={{0,112},{16,0},{32,16},{48,32},{64,48},{80,64},{96,80},{112,96},{1... | collective-permute-start | bytes 786440 | tf_op jit(solution)/shard_map/ppermute | solution.py:119
  63.0 4.8 %copy.19 = bf16[9,32,9,64]{3,2,1,0:T(8,128)(2,1)} copy(bf16[9,32,9,64]{1,2,0,3:T(8,128)(2,1)} %bitcast.26) | data formatting | bytes 663552 | tf_op jit(solution)/shard_map/transpose | solution.py:128
  67.8 0.0 copy-start.3
  67.8 1.9 %reshape.26.a_ref = bf16[288,576]{1,0:T(8,128)(2,1)S(1)} reshape(bf16[9,32,9,64]{3,2,1,0:T(8,128)(2,1)} %copy.19) | data formatting | bytes 663552 | tf_op jit(solution)/shard_map/reshape | solution.py:128
  69.6 0.0 copy-done.3
  69.7 0.1 copy.20.shrink_ref
  69.7 0.5 collective-permute-done.3.up_ref
  70.2 0.5 collective-permute-done.4.down_ref
  70.7 7.1 %shard_map.77 = (bf16[8,32,512]{2,1,0:T(8,128)(2,1)S(1)}, f32[8,9,8,288]{3,2,1,0:T(8,128)}) custom-call(bf16[4,64,512]{2,1,0:T(8,128)(2,1)S(1)} %collective-permute-done.3.up_ref, bf16[8,64,512]{2,1,0:T(8,128)(2,1)S(1)} %all_to_all.16.own_ref, bf16[4,64,512]{2,1,0:T(8,128)(2,1)S(1)} %collective-permute-done.4.down_ref, ...), custom_call_target="tpu_custom_call" | custom-call | tf_op jit(solution)/shard_map/pallas_call | solution.py:152
  77.8 5.4 %all-to-all-start.2 = ((f32[8,9,8,288]{3,2,1,0:T(8,128)}), f32[8,9,8,288]{3,2,1,0:T(8,128)S(1)}, u32[]{:S(2)}, u32[]{:S(2)}) async-start(f32[8,9,8,288]{3,2,1,0:T(8,128)} %get-tuple-element.6), calls=%async_computation.2 | async-start | bytes 1769472 | tf_op jit(solution)/shard_map/all_to_all | solution.py:168
  83.3 1.1 %copy.23 = bf16[64,8,512]{2,1,0:T(8,128)(2,1)} copy(bf16[64,8,512]{2,0,1:T(8,128)(2,1)S(1)} %bitcast.20) | data formatting | bytes 1048576
  84.4 0.9 copy.22
  85.2 11.0 %all-to-all-done.2 = f32[8,9,8,288]{3,2,1,0:T(8,128)S(1)} async-done(((f32[8,9,8,288]{3,2,1,0:T(8,128)}), f32[8,9,8,288]{3,2,1,0:T(8,128)S(1)}, u32[]{:S(2)}, u32[]{:S(2)}) %all-to-all-start.2) | async-done | bytes 663584 | tf_op jit(solution)/shard_map/all_to_all | solution.py:168
  96.2 0.1 reduce_sum.19
  96.3 0.1 reshape.27
  96.4 0.2 copy.21
  96.7 0.8 copy.24
  (4 shorter events, 0.1 us)
Async XLA Ops:
  0.6 42.2 %copy-start = (bf16[64,8,512]{2,1,0:T(8,128)(2,1)S(1)}, bf16[64,8,512]{2,1,0:T(8,128)(2,1)}, u32[]{:S(2)}) copy-start(bf16[64,8,512]{2,1,0:T(8,128)(2,1)} %param.5) | copy-start | bytes 1572868
  0.6 8.8 %copy-start.2 = (bf16[32,5184]{1,0:T(8,128)(2,1)S(1)}, bf16[32,5184]{1,0:T(8,128)(2,1)}, u32[]{:S(2)}) copy-start(bf16[32,5184]{1,0:T(8,128)(2,1)} %param.7) | copy-start | bytes 995332
  2.4 21.6 %collective-permute-start = (bf16[4,32,512]{2,1,0:T(8,128)(2,1)}, bf16[4,32,512]{2,1,0:T(8,128)(2,1)S(1)}, u32[]{:S(2)}, u32[]{:S(2)}) collective-permute-start(bf16[4,32,512]{2,1,0:T(8,128)(2,1)} %get-tuple-element.16), channel_id=1, source_target_pairs={{0,16},{16,32},{32,48},{48,64},{64,80},{80,96},{96,112},{112,0},{1... | collective-permute-start | bytes 393224 | tf_op jit(solution)/shard_map/ppermute | solution.py:118
  5.5 18.5 %collective-permute-start.1 = (bf16[4,32,512]{2,1,0:T(8,128)(2,1)S(1)}, bf16[4,32,512]{2,1,0:T(8,128)(2,1)S(1)}, u32[]{:S(2)}, u32[]{:S(2)}) collective-permute-start(bf16[4,32,512]{2,1,0:T(8,128)(2,1)S(1)} %get-tuple-element.15), channel_id=1, source_target_pairs={{0,112},{16,0},{32,16},{48,32},{64,48},{80,64},{96,80},{112,96},{1... | collective-permute-start | bytes 393224 | tf_op jit(solution)/shard_map/ppermute | solution.py:119
  13.5 6.0 %copy-start.1 = (bf16[32,64,9,9]{0,3,2,1:T(8,128)(2,1)}, bf16[32,64,9,9]{0,3,2,1:T(8,128)(2,1)S(1)}, u32[]{:S(2)}) copy-start(bf16[32,64,9,9]{0,3,2,1:T(8,128)(2,1)S(1)} %reshape.24) | copy-start | bytes 995332
  42.7 1.4 %collective-permute-start.2 = (f32[64,512]{1,0:T(8,128)S(1)}, f32[64,512]{1,0:T(8,128)S(1)}, u32[]{:S(2)}, u32[]{:S(2)}) collective-permute-start(f32[64,512]{1,0:T(8,128)S(1)} %convert_reduce_fusion), channel_id=1, source_target_pairs={{0,1},{1,0},{2,3},{3,2},{4,5},{5,4},{6,7},{7,6},{8,9},{9,8},{10,11... | collective-permute-start | bytes 393224 | tf_op jit(solution)/shard_map/ppermute | solution.py:144
  57.3 12.9 %collective-permute-start.3 = (bf16[4,64,512]{2,1,0:T(8,128)(2,1)S(1)}, bf16[4,64,512]{2,1,0:T(8,128)(2,1)S(1)}, u32[]{:S(2)}, u32[]{:S(2)}) collective-permute-start(bf16[4,64,512]{2,1,0:T(8,128)(2,1)S(1)} %get-tuple-element.14), channel_id=1, source_target_pairs={{0,16},{16,32},{32,48},{48,64},{64,80},{80,96},{96,112},{112,0},{1... | collective-permute-start | bytes 786440 | tf_op jit(solution)/shard_map/ppermute | solution.py:118
  58.0 12.7 %collective-permute-start.4 = (bf16[4,64,512]{2,1,0:T(8,128)(2,1)S(1)}, bf16[4,64,512]{2,1,0:T(8,128)(2,1)S(1)}, u32[]{:S(2)}, u32[]{:S(2)}) collective-permute-start(bf16[4,64,512]{2,1,0:T(8,128)(2,1)S(1)} %get-tuple-element.13), channel_id=1, source_target_pairs={{0,112},{16,0},{32,16},{48,32},{64,48},{80,64},{96,80},{112,96},{1... | collective-permute-start | bytes 786440 | tf_op jit(solution)/shard_map/ppermute | solution.py:119
  67.8 1.9 %copy-start.3 = (f32[32]{0:T(128)S(1)}, f32[32]{0:T(128)}, u32[]{:S(2)}) copy-start(f32[32]{0:T(128)} %param.8) | copy-start | bytes 388
  77.8 18.4 %all-to-all-start.2 = ((f32[8,9,8,288]{3,2,1,0:T(8,128)}), f32[8,9,8,288]{3,2,1,0:T(8,128)S(1)}, u32[]{:S(2)}, u32[]{:S(2)}) async-start(f32[8,9,8,288]{3,2,1,0:T(8,128)} %get-tuple-element.6), calls=%async_computation.2 | async-start | bytes 1769472 | tf_op jit(solution)/shard_map/all_to_all | solution.py:168
where the time goes:
time: 98.6 us; the launch traced here: 97.4 us
  blocking collectives  28.6 us (29%)
  local copies, waits for them, and re-layouts  25.6 us (26%)
  starting transfers between devices  16.9 us (17%)
  waiting for transfers between devices  13.1 us (13%)
  Pallas kernels  9.99 us (10%)
  other arithmetic  2.39 us (2%)
    all_to_all x2, blocking collectives, exchange(): lax.all_to_all(field, 'atom', 0, 0, tiled=True, axis_index_groups=chips)  28.6 us
    all_to_all x1, waiting for transfers between devices, per_device(): got = lax.all_to_all(terms, 'tile', 0, 0, tiled=True)  11 us
    ppermute x2, starting transfers between devices, halos(): down = lax.ppermute(field[:HALO], 'tile', backward)  7.55 us
    pallas_call x1, Pallas kernels, per_device(): pl.pallas_call(functools.partial(update_kernel, scale=scale), out_shape=(...  7.11 us
    transpose x1, local copies, waits for them, and re-layouts, per_device(): a_synth = kernel.transpose(2, 1, 3, 0).reshape(TAP * C, TAP * atoms)  5.95 us
    all_to_all x1, starting transfers between devices, per_device(): got = lax.all_to_all(terms, 'tile', 0, 0, tiled=True)  5.44 us
    unnamed x13, local copies, waits for them, and re-layouts  5.4 us
    transpose x1, local copies, waits for them, and re-layouts, per_device(): a_corr = kernel.transpose(2, 0, 3, 1).reshape(TAP * atoms, TAP * C)  4.79 us
  transfers between devices with their start and end apart: 6, of which 4 were waited for; matrix products, arithmetic and copies ran while one was open for 25% of the time, Pallas kernels for 0%

commit v1 on v0

v1 whole, which is shorter than its diff:
```python
import functools

import jax
import jax.numpy as jnp
from jax import lax
from jax.experimental import pallas as pl
from jax.experimental.pallas import tpu as pltpu
from jax.sharding import PartitionSpec as P

C = 64
TAP = 9
TAPS = TAP * TAP
TILE_W = 512
HALO = TAP // 2
LEFT = 128 - HALO
HALF = C // 2
ROWS = 8
TAP_ROWS = 88
LANES = 384
SHRINK_TERMS = 2.0**-5

step_size = 0.1
eps_sq = 0.01


def shifted(row, j):
    zero = jnp.zeros((row.shape[0], 128), row.dtype)
    wide = jnp.concatenate([zero, row, zero], axis=1)
    return wide[:, LEFT + j : LEFT + j + TILE_W]


def synthesis_kernel(
    core_ref, coef_ref, d_ref, wup_ref, wdown_ref,
    keep_ref, send_ref, acorr_ref,
    by_band, by_atom, turned, asynth, cols, acc,
):
    atoms = coef_ref.shape[1]
    d = d_ref[...].astype(jnp.float32)
    for c in range(C):
        by_band[c * atoms : (c + 1) * atoms, 0:TAPS] = d[:, c * TAPS : (c + 1) * TAPS]
    for k in range(atoms):
        block = by_band[pl.ds(k, C, stride=atoms), :]
        by_atom[k * TAP_ROWS : (k + 1) * TAP_ROWS, 0:C] = jnp.transpose(block)[0:TAP_ROWS, :]
    for tap in range(TAPS):
        dy, dx = divmod(tap, TAP)
        block = by_atom[pl.ds(tap, atoms, stride=TAP_ROWS), :][:, 0:C]
        acorr_ref[dy * atoms : (dy + 1) * atoms, dx * C : (dx + 1) * C] = block.astype(jnp.bfloat16)
        turned[dx * atoms : (dx + 1) * atoms, dy * C : (dy + 1) * C] = block
    asynth[...] = jnp.transpose(turned[...]).astype(jnp.bfloat16)

    acc[...] = jnp.zeros_like(acc)

    def add(slot, q, low, high):
        dy = low - (ROWS - 1) + q
        count = high - low + 1
        acc[low * C : (high + 1) * C, :] += jnp.dot(
            asynth[dy * C : (dy + count) * C, :], cols[slot], preferred_element_type=jnp.float32
        )

    for q in range(ROWS):
        row = coef_ref[q]
        weight = wup_ref[...] if q < HALO else wdown_ref[...]
        for slot, field in ((0, row), (1, row * weight)):
            for dx in range(TAP):
                cols[slot, dx * atoms : (dx + 1) * atoms, :] = shifted(field, dx)
        low, high = ROWS - 1 - q, ROWS + TAP - 2 - q
        add(0, q, max(HALO, low), min(HALO + ROWS - 1, high))
        if q < HALO:
            add(1, q, HALO + ROWS, high)
        else:
            add(1, q, low, HALO - 1)
    core = core_ref[0]
    mine = pl.multiple_of(core * HALF, HALF)
    other = pl.multiple_of((1 - core) * HALF, HALF)
    for j in range(ROWS):
        edge = HALO + ROWS + (HALO - 1) - j if j < HALO else ROWS - 1 - j
        for part, at in ((0, HALO + ROWS - 1 - j), (1, edge)):
            keep_ref[j, part] = acc[pl.ds(at * C + mine, HALF), :]
            send_ref[j, part] = acc[pl.ds(at * C + other, HALF), :].astype(send_ref.dtype)


def pad_row(core, mine_ref, other_ref, wup_ref, wdown_ref, r):
    if r < HALO:
        at, part = r, 1
    elif r < HALO + ROWS:
        at, part = r - HALO, 0
    else:
        at, part = r - ROWS, 1
    mine, other = mine_ref[at, part], other_ref[at, part]
    first = core == 0
    row = jnp.concatenate(
        [jnp.where(first, mine, other), jnp.where(first, other, mine)], axis=0
    )
    if r < HALO:
        return row * wup_ref[...]
    if r >= HALO + ROWS:
        return row * wdown_ref[...]
    return row


def met(r):
    first, last = max(0, r - (TAP - 1)), min(ROWS - 1, r)
    return first, last, first + TAP - 1 - r, last + TAP - 1 - r


def terms_kernel(
    core_ref, mine_ref, other_ref, wup_ref, wdown_ref, coef_ref, term_ref, cols, grad, scale
):
    atoms = coef_ref.shape[1]
    core = core_ref[0]
    grad[...] = jnp.zeros_like(grad)
    for r in range(ROWS + TAP - 1):
        row = pad_row(core, mine_ref, other_ref, wup_ref, wdown_ref, r)
        slot = r % 2
        for dx in range(TAP):
            cols[slot, dx * C : (dx + 1) * C, :] = shifted(row, TAP - 1 - dx)
        first, last, low, high = met(r)
        grad[low * atoms : (high + 1) * atoms, :] += lax.dot_general(
            coef_ref[first : last + 1].reshape((last - first + 1) * atoms, TILE_W),
            cols[slot],
            (((1,), (1,)), ((), ())),
            preferred_element_type=jnp.float32,
        )
    turned = jnp.transpose(grad[...]) * scale
    parts = term_ref.shape[0]
    per = C // parts
    term_ref[...] = jnp.zeros_like(term_ref)
    for dx in range(TAP):
        for t in range(parts):
            term_ref[t, dx * per : (dx + 1) * per, 0 : TAP * atoms] = turned[
                dx * C + t * per : dx * C + (t + 1) * per, :
            ].astype(term_ref.dtype)


def coeffs_kernel(
    core_ref, mine_ref, other_ref, wup_ref, wdown_ref, coef_ref, a_ref, shrink_ref,
    new_ref, cols, acc,
):
    atoms = coef_ref.shape[1]
    core = core_ref[0]
    acc[...] = jnp.zeros_like(acc)
    for r in range(ROWS + TAP - 1):
        row = pad_row(core, mine_ref, other_ref, wup_ref, wdown_ref, r)
        slot = r % 2
        for dx in range(TAP):
            cols[slot, dx * C : (dx + 1) * C, :] = shifted(row, TAP - 1 - dx)
        first, last, low, high = met(r)
        acc[first * atoms : (last + 1) * atoms, :] += jnp.dot(
            a_ref[low * atoms : (high + 1) * atoms, :], cols[slot], preferred_element_type=jnp.float32
        )
    for y in range(ROWS):
        u = coef_ref[y].astype(jnp.float32) + step_size * acc[y * atoms : (y + 1) * atoms, :]
        new_ref[y] = (u - shrink_ref[...] * u / jnp.sqrt(u * u + eps_sq)).astype(new_ref.dtype)


VMEM = pl.BlockSpec(memory_space=pltpu.VMEM)
SMEM = pl.BlockSpec(memory_space=pltpu.SMEM)


def per_device(image, coeffs, dictionary, shrink, seam_map):
    atoms = coeffs.shape[0]
    strips = lax.axis_size("tile")
    groups = lax.axis_size("atom")
    position = lax.axis_index("tile")
    atom_at = lax.axis_index("atom")
    member = atom_at // 2
    core = atom_at % 2
    core_at = core.astype(jnp.int32)[None]
    seam_float = seam_map.astype(jnp.float32)
    w_down = (0.5 + 0.5 * seam_float[position]).astype(jnp.bfloat16)[None, :]
    w_up = (0.5 + 0.5 * seam_float[(position + strips - 1) % strips]).astype(jnp.bfloat16)[None, :]
    chips = [[i for i in range(groups) if i % 2 == side] for side in range(2)]
    swap = [(i, i ^ 1) for i in range(groups)]
    half = groups // 2
    pairs = []
    for s in range(strips):
        for a in range(groups):
            if a < half:
                pairs.append((s * groups + a, (s + strips - 1) % strips * groups + a + half))
            else:
                pairs.append((s * groups + a, (s + 1) % strips * groups + a - half))

    def exchange(field):
        return lax.all_to_all(field, "atom", 0, 0, tiled=True, axis_index_groups=chips)

    coef_rows = coeffs.transpose(1, 0, 2)
    params = pltpu.CompilerParams(vmem_limit_bytes=48 * 1024 * 1024)
    flops = 2 * 72 * atoms * C * TAP * TILE_W
    cost = pl.CostEstimate(flops=flops, bytes_accessed=3 << 20, transcendentals=0)
    keep, send, a_corr = pl.pallas_call(
        synthesis_kernel,
        out_shape=(
            jax.ShapeDtypeStruct((ROWS, 2, HALF, TILE_W), jnp.float32),
            jax.ShapeDtypeStruct((ROWS, 2, HALF, TILE_W), jnp.float32),
            jax.ShapeDtypeStruct((TAP * atoms, TAP * C), jnp.bfloat16),
        ),
        in_specs=[SMEM] + [VMEM] * 4,
        out_specs=(VMEM,) * 3,
        scratch_shapes=[
            pltpu.VMEM((C * atoms, 128), jnp.float32),
            pltpu.VMEM((atoms * TAP_ROWS, 128), jnp.float32),
            pltpu.VMEM((TAP * atoms, TAP * C), jnp.float32),
            pltpu.VMEM((TAP * C, TAP * atoms), jnp.bfloat16),
            pltpu.VMEM((2, TAP * atoms, TILE_W), jnp.bfloat16),
            pltpu.VMEM((2 * ROWS * C, TILE_W), jnp.float32),
        ],
        compiler_params=params,
        cost_estimate=cost,
    )(core_at, coef_rows, dictionary, w_up, w_down)
    other = lax.ppermute(send.astype(jnp.float16), "atom", swap)
    pieces = exchange((keep + other.astype(jnp.float32)).astype(jnp.float16))
    total = jnp.sum(pieces.astype(jnp.float32), axis=0)
    image_row = lax.dynamic_slice(image, (core * HALF, member, 0), (HALF, 1, TILE_W))[:, 0]
    held = jnp.stack([image_row.astype(jnp.float32) - total[0], total[1]])
    facing = lax.ppermute(held, ("tile", "atom"), pairs)
    rows_two = jnp.stack([held[0] - facing[1], facing[0] - held[1]]).astype(jnp.bfloat16)
    mine = exchange(jnp.broadcast_to(rows_two[None], (ROWS, 2, HALF, TILE_W)))
    theirs = lax.ppermute(mine, "atom", swap)

    scale = float((ROWS * strips * TILE_W) ** -0.5) * SHRINK_TERMS
    per = C // strips
    terms = pl.pallas_call(
        functools.partial(terms_kernel, scale=scale),
        out_shape=jax.ShapeDtypeStruct((strips, TAP * per, LANES), jnp.float32),
        in_specs=[SMEM] + [VMEM] * 5,
        out_specs=VMEM,
        scratch_shapes=[
            pltpu.VMEM((2, TAP * C, TILE_W), jnp.bfloat16),
            pltpu.VMEM((TAP * atoms, TAP * C), jnp.float32),
        ],
        compiler_params=params,
        cost_estimate=cost,
    )(core_at, mine, theirs, w_up, w_down, coef_rows)
    got = lax.all_to_all(terms.astype(jnp.float16), "tile", 0, 0, tiled=True)
    new_rows = pl.pallas_call(
        coeffs_kernel,
        out_shape=jax.ShapeDtypeStruct((ROWS, atoms, TILE_W), jnp.bfloat16),
        in_specs=[SMEM] + [VMEM] * 7,
        out_specs=VMEM,
        scratch_shapes=[
            pltpu.VMEM((2, TAP * C, TILE_W), jnp.bfloat16),
            pltpu.VMEM((ROWS * atoms, TILE_W), jnp.float32),
        ],
        compiler_params=params,
        cost_estimate=cost,
    )(core_at, mine, theirs, w_up, w_down, coef_rows, a_corr, shrink[:, None])
    new_coeffs = new_rows.transpose(1, 0, 2)
    own_half, other_half = mine[:, 0], theirs[:, 0]
    residual = jnp.concatenate(
        [
            jnp.where(core == 0, own_half, other_half),
            jnp.where(core == 0, other_half, own_half),
        ],
        axis=1,
    ).transpose(1, 0, 2)
    step = jnp.sum(got.astype(jnp.float32), axis=0)[:, : TAP * atoms] * (1.0 / SHRINK_TERMS)
    step = step.reshape(TAP, per, TAP, atoms)
    atom_step = step.transpose(3, 1, 2, 0).reshape(atoms, per * TAPS)
    return (new_coeffs, residual, atom_step)


def solution(mesh):
    placed = (P(None, "tile", None), P("atom", "tile", None), P("atom", None), P("atom"), P())
    return jax.shard_map(
        per_device,
        mesh=mesh,
        in_specs=placed,
        out_specs=(P("atom", "tile", None), P(None, "tile", None), P("atom", "tile")),
        check_vma=False,
    )
```

time: 98.6 us -> 73.4 us (0.74)
  local copies, waits for them, and re-layouts: 25.6 us -> 5 us
  blocking collectives: 28.6 us -> 12.3 us
  waiting for transfers between devices: 13.1 us -> 21.6 us
  Pallas kernels: 9.99 us -> 11.7 us
  starting transfers between devices: 16.9 us -> 18.6 us
    all_to_all x2 -> x1, blocking collectives: 28.6 us -> 12.3 us  [exchange(): lax.all_to_all(field, 'atom', 0, 0, tiled=True, axis_index_groups=chips)]
    transpose x3 -> x1, local copies, waits for them, and re-layouts: 10.9 us -> 0.21 us  [per_device(): atom_step = step.transpose(3, 1, 2, 0).reshape(atoms, per * TAPS)]
    reshape x6 -> x2, local copies, waits for them, and re-layouts: 8.3 us -> 0.16 us  [the longest x1 0.12 us: per_device(): step = step.reshape(TAP, per, TAP, atoms)]
    all_to_all x1 -> x2, starting transfers between devices: 5.44 us -> 13.5 us  [the longest x1 7.18 us: per_device(): got = lax.all_to_all(terms.astype(jnp.float16), 'tile', 0, 0, tiled=True)]
    ppermute x5 -> x3, starting transfers between devices: 11.4 us -> 5.09 us  [the longest x1 5.01 us: per_device(): facing = lax.ppermute(held, ('tile', 'atom'), pairs)]
    ppermute x5 -> x3, waiting for transfers between devices: 2.14 us -> 6.43 us  [the longest x1 3.37 us: per_device(): facing = lax.ppermute(held, ('tile', 'atom'), pairs)]
    all_to_all x1 -> x2, waiting for transfers between devices: 11 us -> 15.2 us  [the longest x1 9.64 us: exchange(): lax.all_to_all(field, 'atom', 0, 0, tiled=True, axis_index_groups=chips)]
    convert_element_type x2 -> x3, other arithmetic: 0.13 us -> 1.92 us  [the longest x1 1 us: per_device(): pieces = exchange((keep + other.astype(jnp.float32)).astype(jnp.float16))]
  transfers between devices with their start and end apart: 6 -> 5, of which waited for: 4 -> 5; matrix products, arithmetic and copies ran while one was open for 25% -> 3% of each run, Pallas kernels for 0% -> 5%
where the time goes in v1:
time: 73.4 us; the launch traced here: 73 us
  waiting for transfers between devices  21.6 us (29%)
  starting transfers between devices  18.6 us (25%)
  blocking collectives  12.3 us (17%)
  Pallas kernels  11.7 us (16%)
  local copies, waits for them, and re-layouts  5 us (7%)
  other arithmetic  3.04 us (4%)
  between operations  0.84 us (1%)
    all_to_all x1, blocking collectives, exchange(): lax.all_to_all(field, 'atom', 0, 0, tiled=True, axis_index_groups=chips)  12.3 us
    all_to_all x1, waiting for transfers between devices, exchange(): lax.all_to_all(field, 'atom', 0, 0, tiled=True, axis_index_groups=chips)  9.64 us
    all_to_all x1, starting transfers between devices, per_device(): got = lax.all_to_all(terms.astype(jnp.float16), 'tile', 0, 0, tiled=True)  7.18 us
    all_to_all x1, starting transfers between devices, exchange(): lax.all_to_all(field, 'atom', 0, 0, tiled=True, axis_index_groups=chips)  6.34 us
    all_to_all x1, waiting for transfers between devices, per_device(): got = lax.all_to_all(terms.astype(jnp.float16), 'tile', 0, 0, tiled=True)  5.54 us
    ppermute x1, starting transfers between devices, per_device(): facing = lax.ppermute(held, ('tile', 'atom'), pairs)  5.01 us
    pallas_call x1, Pallas kernels, per_device(): pl.pallas_call(synthesis_kernel, out_shape=(jax.ShapeDtypeStruct((ROWS, 2...  4.47 us
    unnamed x10, local copies, waits for them, and re-layouts  4.42 us
  transfers between devices with their start and end apart: 5, of which 5 were waited for; matrix products, arithmetic and copies ran while one was open for 3% of the time, Pallas kernels for 5%

profile of v1, /device:TPU:0, one launch (start us, length us, event | category | flops | bytes accessed | tf_op | source)
XLA Modules:
  0.0 73.0 jit_solution(84843483307872506)
XLA Ops:
  0.6 0.0 copy-start
  0.6 0.0 copy-start.1
  0.7 0.8 %convert_element_type.50 = f32[8,512]{1,0:T(8,128)S(1)} convert(s32[8,512]{1,0:T(8,128)} %param.9) | non-fusion elementwise | flops 4096 | bytes 32768 | tf_op jit(solution)/shard_map/convert_element_type | solution.py:169
  1.5 1.0 %copy.49 = bf16[32,8,512]{2,0,1:T(8,128)(2,1)S(1)} copy(bf16[32,8,512]{2,1,0:T(8,128)(2,1)} %param.6) | data formatting | bytes 524288 | tf_op args[1]
  2.5 0.0 copy-done.1
  2.6 4.5 %shard_map.76 = (f32[8,2,32,512]{3,2,1,0:T(8,128)S(1)}, f32[8,2,32,512]{3,2,1,0:T(8,128)S(1)}, bf16[288,576]{1,0:T(8,128)(2,1)S(1)}) custom-call(s32[1]{0:T(128)} %bitcast.core_ref, bf16[8,32,512]{2,1,0:T(8,128)(2,1)S(1)} %bitcast.32, bf16[32,5184]{1,0:T(8,128)(2,1)S(1)} %copy-done.1, bf16[1,512]{1,0:T(2,128)(2,1)S(1)} %get-tuple-element.23.wup_ref, ...), custom_call_target="tpu_custom_call" | custom-call | flops 1358954496 | bytes 3145728 | tf_op jit(solution)/shard_map/pallas_call | solution.py:190
  7.0 0.1 convert_element_type.53
  7.1 0.1 collective-permute-start
  7.2 1.9 %collective-permute-done = f16[8,2,32,512]{3,2,1,0:T(8,128)(2,1)S(1)} collective-permute-done((f16[8,2,32,512]{3,2,1,0:T(8,128)(2,1)S(1)}, f16[8,2,32,512]{3,2,1,0:T(8,128)(2,1)S(1)}, u32[]{:S(2)}, u32[]{:S(2)}) %collective-permute-start) | collective-permute-done | bytes 524320 | tf_op jit(solution)/shard_map/ppermute | solution.py:210
  9.1 1.0 %add_convert_fusion = f16[8,2,32,512]{3,2,1,0:T(8,128)(2,1)} fusion(f32[8,2,32,512]{3,2,1,0:T(8,128)S(1)} %get-tuple-element.6, f16[8,2,32,512]{3,2,1,0:T(8,128)(2,1)S(1)} %collective-permute-done), kind=kLoop, calls=%fused_computation.1 | loop fusion | flops 786432 | bytes 2097152 | tf_op jit(solution)/shard_map/convert_element_type | solution.py:211
  10.1 6.3 %all-to-all-start = ((f16[8,2,32,512]{3,2,1,0:T(8,128)(2,1)}), f16[8,2,32,512]{3,2,1,0:T(8,128)(2,1)S(1)}, u32[]{:S(2)}, u32[]{:S(2)}) async-start(f16[8,2,32,512]{3,2,1,0:T(8,128)(2,1)} %add_convert_fusion), calls=%async_computation | async-start | bytes 1048576 | tf_op jit(solution)/shard_map/all_to_all | solution.py:184
  16.5 0.0 copy-done
  16.5 0.1 constant_dynamic-slice_fusion
  16.6 9.6 %all-to-all-done = f16[8,2,32,512]{3,2,1,0:T(8,128)(2,1)S(1)} async-done(((f16[8,2,32,512]{3,2,1,0:T(8,128)(2,1)}), f16[8,2,32,512]{3,2,1,0:T(8,128)(2,1)S(1)}, u32[]{:S(2)}, u32[]{:S(2)}) %all-to-all-start) | async-done | bytes 524320 | tf_op jit(solution)/shard_map/all_to_all | solution.py:184
  26.2 0.1 convert_reduce_fusion
  26.3 5.0 %collective-permute-start.1 = (f32[2,32,512]{2,1,0:T(8,128)S(1)}, f32[2,32,512]{2,1,0:T(8,128)S(1)}, u32[]{:S(2)}, u32[]{:S(2)}) collective-permute-start(f32[2,32,512]{2,1,0:T(8,128)S(1)} %pad_maximum_fusion), channel_id=1, source_target_pairs={{0,120},{1,121},{2,122},{3,123},{4,124},{5,125},{6,126},{7,127},{8... | collective-permute-start | bytes 393224 | tf_op jit(solution)/shard_map/ppermute | solution.py:215
  31.3 3.4 %collective-permute-done.1 = f32[2,32,512]{2,1,0:T(8,128)S(1)} collective-permute-done((f32[2,32,512]{2,1,0:T(8,128)S(1)}, f32[2,32,512]{2,1,0:T(8,128)S(1)}, u32[]{:S(2)}, u32[]{:S(2)}) %collective-permute-start.1) | collective-permute-done | bytes 131104 | tf_op jit(solution)/shard_map/ppermute | solution.py:215
  34.8 12.3 %all_to_all.15.mine_ref = bf16[8,2,32,512]{3,2,1,0:T(8,128)(2,1)S(1)} all-to-all(bf16[8,2,32,512]{3,2,1,0:T(8,128)(2,1)S(1)} %broadcast_in_dim.7), channel_id=1, replica_groups={{0,2,4,6,8,10,12,14},{1,3,5,7,9,11,13,15},{16,18,20,22,24,26,28,30},{17..., dimensions={0} | all-to-all | bytes 1048576 | tf_op jit(solution)/shard_map/all_to_all | solution.py:184
  47.1 0.0 collective-permute-start.2
  47.1 0.0 copy-start.2
  47.1 0.7 copy-done.2
  47.7 0.1 copy.34.shrink_ref
  47.8 1.2 %collective-permute-done.2.other_ref = bf16[8,2,32,512]{3,2,1,0:T(8,128)(2,1)S(1)} collective-permute-done((bf16[8,2,32,512]{3,2,1,0:T(8,128)(2,1)S(1)}, bf16[8,2,32,512]{3,2,1,0:T(8,128)(2,1)S(1)}, u32[]{:S(2)}, u32[]{:S(2)}) %collective-permute-start.2) | collective-permute-done | bytes 524320 | tf_op jit(solution)/shard_map/ppermute | solution.py:218
  49.0 3.8 %shard_map.78 = f32[8,72,384]{2,1,0:T(8,128)S(1)} custom-call(s32[1]{0:T(128)} %bitcast.core_ref, bf16[8,2,32,512]{3,2,1,0:T(8,128)(2,1)S(1)} %all_to_all.15.mine_ref, bf16[8,2,32,512]{3,2,1,0:T(8,128)(2,1)S(1)} %collective-permute-done.2.other_ref, bf16[1,512]{1,0:T(2,128)(2,1)S(1)} %get-tuple-element.23.wup_ref, ...), custom_call_target="tpu_custom_call" | custom-call | flops 1358954496 | bytes 3145728 | tf_op jit(solution)/shard_map/pallas_call | solution.py:222
  52.8 0.8 %convert_element_type.57 = f16[8,72,384]{2,1,0:T(8,128)(2,1)} convert(f32[8,72,384]{2,1,0:T(8,128)S(1)} %shard_map.78) | non-fusion elementwise | flops 221184 | bytes 1327104 | tf_op jit(solution)/shard_map/convert_element_type | solution.py:234
  53.6 7.2 %all-to-all-start.2 = ((f16[8,72,384]{2,1,0:T(8,128)(2,1)}), f16[8,72,384]{2,1,0:T(8,128)(2,1)S(1)}, u32[]{:S(2)}, u32[]{:S(2)}) async-start(f16[8,72,384]{2,1,0:T(8,128)(2,1)} %convert_element_type.57), calls=%async_computation.2 | async-start | bytes 884736 | tf_op jit(solution)/shard_map/all_to_all | solution.py:234
  60.9 1.1 %copy.41 = bf16[64,8,512]{2,1,0:T(8,128)(2,1)} copy(bf16[64,8,512]{2,0,1:T(8,128)(2,1)S(1)} %maximum_bitcast_fusion) | data formatting | bytes 1048576
  61.9 3.4 %shard_map.77 = bf16[8,32,512]{2,1,0:T(8,128)(2,1)S(1)} custom-call(s32[1]{0:T(128)} %bitcast.core_ref, bf16[8,2,32,512]{3,2,1,0:T(8,128)(2,1)S(1)} %all_to_all.15.mine_ref, bf16[8,2,32,512]{3,2,1,0:T(8,128)(2,1)S(1)} %collective-permute-done.2.other_ref, bf16[1,512]{1,0:T(2,128)(2,1)S(1)} %get-tuple-element.23.wup_ref, ...), custom_call_target="tpu_custom_call" | custom-call | flops 1358954496 | bytes 3145728 | tf_op jit(solution)/shard_map/pallas_call | solution.py:235
  65.4 0.9 %copy.40 = bf16[32,8,512]{2,1,0:T(8,128)(2,1)} copy(bf16[32,8,512]{2,0,1:T(8,128)(2,1)S(1)} %bitcast.35) | data formatting | bytes 524288
  66.2 5.5 %all-to-all-done.2 = f16[8,72,384]{2,1,0:T(8,128)(2,1)S(1)} async-done(((f16[8,72,384]{2,1,0:T(8,128)(2,1)}), f16[8,72,384]{2,1,0:T(8,128)(2,1)S(1)}, u32[]{:S(2)}, u32[]{:S(2)}) %all-to-all-start.2) | async-done | bytes 442400 | tf_op jit(solution)/shard_map/all_to_all | solution.py:234
  71.8 0.1 convert_reduce_fusion.1
  71.8 0.1 reshape.44
  72.0 0.2 copy.39
  72.2 0.8 %copy.42 = f32[32,648]{1,0:T(8,128)} copy(f32[32,648]{0,1:T(8,128)S(1)} %reshape.45) | data formatting | bytes 165888
  (11 shorter events, 0.3 us)
Async XLA Ops:
  0.6 15.9 %copy-start = (bf16[64,8,512]{2,1,0:T(8,128)(2,1)S(1)}, bf16[64,8,512]{2,1,0:T(8,128)(2,1)}, u32[]{:S(2)}) copy-start(bf16[64,8,512]{2,1,0:T(8,128)(2,1)} %param.5) | copy-start | bytes 1572868
  0.6 1.9 %copy-start.1 = (bf16[32,5184]{1,0:T(8,128)(2,1)S(1)}, bf16[32,5184]{1,0:T(8,128)(2,1)}, u32[]{:S(2)}) copy-start(bf16[32,5184]{1,0:T(8,128)(2,1)} %d_ref.1) | copy-start | bytes 995332
  7.1 2.0 %collective-permute-start = (f16[8,2,32,512]{3,2,1,0:T(8,128)(2,1)S(1)}, f16[8,2,32,512]{3,2,1,0:T(8,128)(2,1)S(1)}, u32[]{:S(2)}, u32[]{:S(2)}) collective-permute-start(f16[8,2,32,512]{3,2,1,0:T(8,128)(2,1)S(1)} %convert_element_type.53), channel_id=1, source_target_pairs={{0,1},{1,0},{2,3},{3,2},{4,5},{5,4},{6,7},{7,6},{8,9},{9,8},{10,11... | collective-permute-start | bytes 1572872 | tf_op jit(solution)/shard_map/ppermute | solution.py:210
  10.1 16.1 %all-to-all-start = ((f16[8,2,32,512]{3,2,1,0:T(8,128)(2,1)}), f16[8,2,32,512]{3,2,1,0:T(8,128)(2,1)S(1)}, u32[]{:S(2)}, u32[]{:S(2)}) async-start(f16[8,2,32,512]{3,2,1,0:T(8,128)(2,1)} %add_convert_fusion), calls=%async_computation | async-start | bytes 1048576 | tf_op jit(solution)/shard_map/all_to_all | solution.py:184
  26.3 8.4 %collective-permute-start.1 = (f32[2,32,512]{2,1,0:T(8,128)S(1)}, f32[2,32,512]{2,1,0:T(8,128)S(1)}, u32[]{:S(2)}, u32[]{:S(2)}) collective-permute-start(f32[2,32,512]{2,1,0:T(8,128)S(1)} %pad_maximum_fusion), channel_id=1, source_target_pairs={{0,120},{1,121},{2,122},{3,123},{4,124},{5,125},{6,126},{7,127},{8... | collective-permute-start | bytes 393224 | tf_op jit(solution)/shard_map/ppermute | solution.py:215
  47.1 1.9 %collective-permute-start.2 = (bf16[8,2,32,512]{3,2,1,0:T(8,128)(2,1)S(1)}, bf16[8,2,32,512]{3,2,1,0:T(8,128)(2,1)S(1)}, u32[]{:S(2)}, u32[]{:S(2)}) collective-permute-start(bf16[8,2,32,512]{3,2,1,0:T(8,128)(2,1)S(1)} %all_to_all.15.mine_ref), channel_id=1, source_target_pairs={{0,1},{1,0},{2,3},{3,2},{4,5},{5,4},{6,7},{7,6},{8,9},{9,8},{10,11... | collective-permute-start | bytes 1572872 | tf_op jit(solution)/shard_map/ppermute | solution.py:218
  47.1 0.7 copy-start.2
  53.6 18.2 %all-to-all-start.2 = ((f16[8,72,384]{2,1,0:T(8,128)(2,1)}), f16[8,72,384]{2,1,0:T(8,128)(2,1)S(1)}, u32[]{:S(2)}, u32[]{:S(2)}) async-start(f16[8,72,384]{2,1,0:T(8,128)(2,1)} %convert_element_type.57), calls=%async_computation.2 | async-start | bytes 884736 | tf_op jit(solution)/shard_map/all_to_all | solution.py:234

commit v2 on v1

v2 whole, which is shorter than its diff:
```python
import functools

import jax
import jax.numpy as jnp
from jax import lax
from jax.experimental import pallas as pl
from jax.experimental.pallas import tpu as pltpu
from jax.sharding import PartitionSpec as P

C = 64
TAP = 9
TAPS = TAP * TAP
TILE_W = 512
HALO = TAP // 2
LEFT = 128 - HALO
HALF = C // 2
ROWS = 8
TAP_ROWS = 88
LANES = 384
SHRINK_TERMS = 2.0**-5

step_size = 0.1
eps_sq = 0.01


def seam_weight(seam_ref, at):
    seam = seam_ref[pl.ds(at, 1), :].astype(jnp.float32)
    return (0.5 + 0.5 * seam).astype(jnp.bfloat16)


def turn(block):
    return jnp.swapaxes(block.astype(jnp.float32), 0, 1).astype(jnp.bfloat16)


def shifted(row, j):
    zero = jnp.zeros((row.shape[0], 128), row.dtype)
    wide = jnp.concatenate([zero, row, zero], axis=1)
    return wide[:, LEFT + j : LEFT + j + TILE_W]


def synthesis_kernel(
    coef_hbm, d_hbm, seam_hbm,
    keep_ref, send_ref, acorr_ref, rows_ref, edge_ref,
    coef_ref, d_ref, seam_ref, by_band, by_atom, turned, asynth, cols, acc, sems,
):
    atoms = coef_ref.shape[0]
    copies = [
        pltpu.make_async_copy(source, target, sems.at[i])
        for i, (source, target) in enumerate(
            ((d_hbm, d_ref), (coef_hbm, coef_ref), (seam_hbm, seam_ref))
        )
    ]
    for copy in copies:
        copy.start()
    copies[0].wait()
    d = d_ref[...].astype(jnp.float32)
    for c in range(C):
        by_band[c * atoms : (c + 1) * atoms, 0:TAPS] = d[:, c * TAPS : (c + 1) * TAPS]
    for k in range(atoms):
        block = by_band[pl.ds(k, C, stride=atoms), :]
        by_atom[k * TAP_ROWS : (k + 1) * TAP_ROWS, 0:C] = jnp.transpose(block)[0:TAP_ROWS, :]
    for tap in range(TAPS):
        dy, dx = divmod(tap, TAP)
        block = by_atom[pl.ds(tap, atoms, stride=TAP_ROWS), :][:, 0:C]
        acorr_ref[dy * atoms : (dy + 1) * atoms, dx * C : (dx + 1) * C] = block.astype(jnp.bfloat16)
        turned[dx * atoms : (dx + 1) * atoms, dy * C : (dy + 1) * C] = block
    asynth[...] = jnp.transpose(turned[...]).astype(jnp.bfloat16)

    copies[1].wait()
    copies[2].wait()
    position = lax.axis_index("tile")
    strips = seam_ref.shape[0]
    w_up = seam_weight(seam_ref, lax.rem(position + (strips - 1), strips))
    w_down = seam_weight(seam_ref, position)
    edge_ref[0:1, :] = w_up
    edge_ref[1:2, :] = w_down
    rows_ref[...] = turn(coef_ref[...])
    acc[...] = jnp.zeros_like(acc)

    def add(slot, q, low, high):
        dy = low - (ROWS - 1) + q
        count = high - low + 1
        acc[low * C : (high + 1) * C, :] += jnp.dot(
            asynth[dy * C : (dy + count) * C, :], cols[slot], preferred_element_type=jnp.float32
        )

    for q in range(ROWS):
        row = rows_ref[q]
        weight = w_up if q < HALO else w_down
        for slot, field in ((0, row), (1, row * weight)):
            for dx in range(TAP):
                cols[slot, dx * atoms : (dx + 1) * atoms, :] = shifted(field, dx)
        low, high = ROWS - 1 - q, ROWS + TAP - 2 - q
        add(0, q, max(HALO, low), min(HALO + ROWS - 1, high))
        if q < HALO:
            add(1, q, HALO + ROWS, high)
        else:
            add(1, q, low, HALO - 1)
    core = lax.rem(lax.axis_index("atom"), 2)
    mine = pl.multiple_of(core * HALF, HALF)
    other = pl.multiple_of((1 - core) * HALF, HALF)
    for j in range(ROWS):
        edge = HALO + ROWS + (HALO - 1) - j if j < HALO else ROWS - 1 - j
        for part, at in ((0, HALO + ROWS - 1 - j), (1, edge)):
            keep_ref[j, part] = acc[pl.ds(at * C + mine, HALF), :]
            send_ref[j, part] = acc[pl.ds(at * C + other, HALF), :].astype(send_ref.dtype)


def pad_row(core, mine_ref, other_ref, w_up, w_down, r):
    if r < HALO:
        at, part = r, 1
    elif r < HALO + ROWS:
        at, part = r - HALO, 0
    else:
        at, part = r - ROWS, 1
    mine, other = mine_ref[at, part], other_ref[at, part]
    first = core == 0
    row = jnp.concatenate(
        [jnp.where(first, mine, other), jnp.where(first, other, mine)], axis=0
    )
    if r < HALO:
        return row * w_up
    if r >= HALO + ROWS:
        return row * w_down
    return row


def met(r):
    first, last = max(0, r - (TAP - 1)), min(ROWS - 1, r)
    return first, last, first + TAP - 1 - r, last + TAP - 1 - r


def terms_kernel(half_ref, edge_ref, coef_ref, term_ref, cols, lags, scale):
    atoms = coef_ref.shape[1]
    wide = ROWS * TILE_W
    sums = []
    for part in range(2):
        for i in range(ROWS):
            r = part * ROWS + i
            if r < HALO:
                row = half_ref[r, 1] * edge_ref[0:1, :]
            elif r < HALO + ROWS:
                row = half_ref[r - HALO, 0]
            else:
                row = half_ref[r - ROWS, 1] * edge_ref[1:2, :]
            columns = slice(i * TILE_W, (i + 1) * TILE_W)
            for dx in range(TAP):
                cols[part, dx * HALF : (dx + 1) * HALF, columns] = shifted(row, TAP - 1 - dx)
            for at in range(ROWS):
                y = r - (ROWS - 1) - part + at
                there = 0 <= y < ROWS
                lags[part, at * atoms : (at + 1) * atoms, columns] = (
                    coef_ref[y] if there else jnp.zeros((atoms, TILE_W), jnp.bfloat16)
                )
        sums.append(
            lax.dot_general(
                cols[part], lags[part], (((1,), (1,)), ((), ())), preferred_element_type=jnp.float32
            )
        )
    edge = jnp.zeros((TAP * HALF, atoms), jnp.float32)
    total = jnp.concatenate([edge, sums[0]], axis=1) + jnp.concatenate([sums[1], edge], axis=1)
    total = jnp.concatenate(
        [total * scale, jnp.zeros((TAP * HALF, LANES - TAP * atoms), jnp.float32)], axis=1
    )
    parts = term_ref.shape[0]
    per = HALF // parts
    for dx in range(TAP):
        for t in range(parts):
            term_ref[t, dx * per : (dx + 1) * per, :] = total[
                dx * HALF + t * per : dx * HALF + (t + 1) * per, :
            ]


def coeffs_kernel(
    mine_ref, other_ref, edge_ref, coef_ref, a_ref, shrink_ref,
    new_ref, resid_ref, cols, acc, own,
):
    atoms = coef_ref.shape[1]
    core = lax.rem(lax.axis_index("atom"), 2)
    w_up, w_down = edge_ref[0:1, :], edge_ref[1:2, :]
    acc[...] = jnp.zeros_like(acc)
    for r in range(ROWS + TAP - 1):
        row = pad_row(core, mine_ref, other_ref, w_up, w_down, r)
        if HALO <= r < HALO + ROWS:
            own[r - HALO] = row
        slot = r % 2
        for dx in range(TAP):
            cols[slot, dx * C : (dx + 1) * C, :] = shifted(row, TAP - 1 - dx)
        first, last, low, high = met(r)
        acc[first * atoms : (last + 1) * atoms, :] += jnp.dot(
            a_ref[low * atoms : (high + 1) * atoms, :], cols[slot], preferred_element_type=jnp.float32
        )
    u = coef_ref[...].reshape(ROWS * atoms, TILE_W).astype(jnp.float32) + step_size * acc[...]
    threshold = jnp.concatenate([shrink_ref[...]] * ROWS, axis=0)
    u = u - threshold * u / jnp.sqrt(u * u + eps_sq)
    new_ref[...] = turn(u.reshape(ROWS, atoms, TILE_W))
    resid_ref[...] = turn(own[...])


VMEM = pl.BlockSpec(memory_space=pltpu.VMEM)
HBM = pl.BlockSpec(memory_space=pltpu.HBM)


def per_device(image, coeffs, dictionary, shrink, seam_map):
    atoms = coeffs.shape[0]
    strips = lax.axis_size("tile")
    groups = lax.axis_size("atom")
    atom_at = lax.axis_index("atom")
    member = atom_at // 2
    core = atom_at % 2
    chips = [[i for i in range(groups) if i % 2 == side] for side in range(2)]
    swap = [(i, i ^ 1) for i in range(groups)]
    half = groups // 2
    pairs = []
    for s in range(strips):
        for a in range(groups):
            if a < half:
                pairs.append((s * groups + a, (s + strips - 1) % strips * groups + a + half))
            else:
                pairs.append((s * groups + a, (s + 1) % strips * groups + a - half))

    def exchange(field):
        return lax.all_to_all(field, "atom", 0, 0, tiled=True, axis_index_groups=chips)

    params = pltpu.CompilerParams(vmem_limit_bytes=48 * 1024 * 1024)
    flops = 2 * 72 * atoms * C * TAP * TILE_W
    cost = pl.CostEstimate(flops=flops, bytes_accessed=3 << 20, transcendentals=0)
    keep, send, a_corr, coef_rows, edges = pl.pallas_call(
        synthesis_kernel,
        out_shape=(
            jax.ShapeDtypeStruct((ROWS, 2, HALF, TILE_W), jnp.float32),
            jax.ShapeDtypeStruct((ROWS, 2, HALF, TILE_W), jnp.float32),
            jax.ShapeDtypeStruct((TAP * atoms, TAP * C), jnp.bfloat16),
            jax.ShapeDtypeStruct((ROWS, atoms, TILE_W), jnp.bfloat16),
            jax.ShapeDtypeStruct((2, TILE_W), jnp.bfloat16),
        ),
        in_specs=[HBM] * 3,
        out_specs=(VMEM,) * 5,
        scratch_shapes=[
            pltpu.VMEM(coeffs.shape, jnp.bfloat16),
            pltpu.VMEM(dictionary.shape, jnp.bfloat16),
            pltpu.VMEM(seam_map.shape, jnp.int32),
            pltpu.VMEM((C * atoms, 128), jnp.float32),
            pltpu.VMEM((atoms * TAP_ROWS, 128), jnp.float32),
            pltpu.VMEM((TAP * atoms, TAP * C), jnp.float32),
            pltpu.VMEM((TAP * C, TAP * atoms), jnp.bfloat16),
            pltpu.VMEM((2, TAP * atoms, TILE_W), jnp.bfloat16),
            pltpu.VMEM((2 * ROWS * C, TILE_W), jnp.float32),
            pltpu.SemaphoreType.DMA((3,)),
        ],
        compiler_params=params,
        cost_estimate=cost,
    )(coeffs, dictionary, seam_map)
    image_row = lax.dynamic_slice(image, (core * HALF, member, 0), (HALF, 1, TILE_W))[:, 0]
    other = lax.ppermute(send.astype(jnp.float16), "atom", swap)
    partial = (keep + other.astype(jnp.float32)).astype(jnp.float16)
    partial, image_row, threshold = lax.optimization_barrier((partial, image_row, shrink[:, None]))
    pieces = exchange(partial)
    total = jnp.sum(pieces.astype(jnp.float32), axis=0)
    held = jnp.stack([image_row.astype(jnp.float32) - total[0], total[1]])
    facing = lax.ppermute(held, ("tile", "atom"), pairs)
    rows_two = jnp.stack([held[0] - facing[1], facing[0] - held[1]]).astype(jnp.bfloat16)
    mine = exchange(jnp.broadcast_to(rows_two[None], (ROWS, 2, HALF, TILE_W)))
    theirs = lax.ppermute(mine, "atom", swap)

    scale = float((ROWS * strips * TILE_W) ** -0.5) * SHRINK_TERMS
    per = C // strips
    term_half = pl.pallas_call(
        functools.partial(terms_kernel, scale=scale),
        out_shape=jax.ShapeDtypeStruct((strips // 2, TAP * per, LANES), jnp.float32),
        in_specs=[VMEM] * 3,
        out_specs=VMEM,
        scratch_shapes=[
            pltpu.VMEM((2, TAP * HALF, ROWS * TILE_W), jnp.bfloat16),
            pltpu.VMEM((2, ROWS * atoms, ROWS * TILE_W), jnp.bfloat16),
        ],
        compiler_params=params,
        cost_estimate=pl.CostEstimate(flops=flops // 2, bytes_accessed=3 << 20, transcendentals=0),
    )
    my_terms = term_half(mine, edges, coef_rows)
    their_terms = term_half(theirs, edges, coef_rows)
    first = core == 0
    terms = jnp.concatenate(
        [jnp.where(first, my_terms, their_terms), jnp.where(first, their_terms, my_terms)]
    ).astype(jnp.float16)
    got = lax.all_to_all(terms, "tile", 0, 0, tiled=True)
    new_coeffs, residual = pl.pallas_call(
        coeffs_kernel,
        out_shape=(
            jax.ShapeDtypeStruct((atoms, ROWS, TILE_W), jnp.bfloat16),
            jax.ShapeDtypeStruct((C, ROWS, TILE_W), jnp.bfloat16),
        ),
        in_specs=[VMEM] * 6,
        out_specs=(VMEM,) * 2,
        scratch_shapes=[
            pltpu.VMEM((2, TAP * C, TILE_W), jnp.bfloat16),
            pltpu.VMEM((ROWS * atoms, TILE_W), jnp.float32),
            pltpu.VMEM((ROWS, C, TILE_W), jnp.bfloat16),
        ],
        compiler_params=params,
        cost_estimate=cost,
    )(mine, theirs, edges, coef_rows, a_corr, threshold)
    step = jnp.sum(got.astype(jnp.float32), axis=0)[:, : TAP * atoms] * (1.0 / SHRINK_TERMS)
    step = step.reshape(TAP, per, TAP, atoms)
    atom_step = step.transpose(3, 1, 2, 0).reshape(atoms, per * TAPS)
    return (new_coeffs, residual, atom_step)


def solution(mesh):
    placed = (P(None, "tile", None), P("atom", "tile", None), P("atom", None), P("atom"), P())
    return jax.shard_map(
        per_device,
        mesh=mesh,
        in_specs=placed,
        out_specs=(P("atom", "tile", None), P(None, "tile", None), P("atom", "tile")),
        check_vma=False,
    )
```

time: 73.4 us -> 70.6 us (0.962)
  blocking collectives: 12.3 us -> 27.5 us
  waiting for transfers between devices: 21.6 us -> 12.7 us
  starting transfers between devices: 18.6 us -> 11.3 us
  other arithmetic: 3.04 us -> 1.47 us
  local copies, waits for them, and re-layouts: 5 us -> 4.08 us
    all_to_all x1 -> x2, blocking collectives: 12.3 us -> 27.5 us  [exchange(): lax.all_to_all(field, 'atom', 0, 0, tiled=True, axis_index_groups=chips)]
    all_to_all x2 -> x1, waiting for transfers between devices: 15.2 us -> 6.73 us  [per_device(): got = lax.all_to_all(terms, 'tile', 0, 0, tiled=True)]
    all_to_all x2 -> x1, starting transfers between devices: 13.5 us -> 6.76 us  [per_device(): got = lax.all_to_all(terms, 'tile', 0, 0, tiled=True)]
    convert_element_type x4 -> x1, other arithmetic: 2.64 us -> 0.21 us  [per_device(): partial = (keep + other.astype(jnp.float32)).astype(jnp.float16)]
    unnamed x10 -> x12, local copies, waits for them, and re-layouts: 4.42 us -> 3.5 us
    ppermute x1, waiting for transfers between devices: 1.16 us -> 0.24 us  [per_device(): theirs = lax.ppermute(mine, 'atom', swap)]
    concatenate x0 -> x1, other arithmetic: none -> 0.87 us  [per_device(): jnp.concatenate([jnp.where(first, my_terms, their_terms), jnp.where(first...]
    pallas_call x2 -> x3, Pallas kernels: 7.19 us -> 7.63 us  [the longest x1 4.32 us: per_device(): pl.pallas_call(coeffs_kernel, out_shape=(jax.ShapeDtypeStruct((atoms, ROW...]
  transfers between devices with their start and end apart: 5 -> 4, of which waited for: 5 -> 4; matrix products, arithmetic and copies ran while one was open for 3% -> 0% of each run, Pallas kernels for 5% -> 8%
where the time goes in v2:
time: 70.6 us; the launch traced here: 70.3 us
  blocking collectives  27.5 us (39%)
  waiting for transfers between devices  12.7 us (18%)
  Pallas kernels  12.4 us (18%)
  starting transfers between devices  11.3 us (16%)
  local copies, waits for them, and re-layouts  4.08 us (6%)
  other arithmetic  1.47 us (2%)
  between operations  0.85 us (1%)
    all_to_all x2, blocking collectives, exchange(): lax.all_to_all(field, 'atom', 0, 0, tiled=True, axis_index_groups=chips)  27.5 us
    all_to_all x1, starting transfers between devices, per_device(): got = lax.all_to_all(terms, 'tile', 0, 0, tiled=True)  6.76 us
    all_to_all x1, waiting for transfers between devices, per_device(): got = lax.all_to_all(terms, 'tile', 0, 0, tiled=True)  6.73 us
    pallas_call x1, Pallas kernels, per_device(): pl.pallas_call(synthesis_kernel, out_shape=(jax.ShapeDtypeStruct((ROWS, 2...  4.78 us
    ppermute x1, starting transfers between devices, per_device(): facing = lax.ppermute(held, ('tile', 'atom'), pairs)  4.41 us
    pallas_call x1, Pallas kernels, per_device(): pl.pallas_call(coeffs_kernel, out_shape=(jax.ShapeDtypeStruct((atoms, ROW...  4.32 us
    ppermute x1, waiting for transfers between devices, per_device(): facing = lax.ppermute(held, ('tile', 'atom'), pairs)  3.96 us
    unnamed x12, local copies, waits for them, and re-layouts  3.5 us
  transfers between devices with their start and end apart: 4, of which 4 were waited for; matrix products, arithmetic and copies ran while one was open for 0% of the time, Pallas kernels for 8%

profile of v2, /device:TPU:0, one launch (start us, length us, event | category | flops | bytes accessed | tf_op | source)
XLA Modules:
  0.0 70.3 jit_solution(17682072375094380749)
XLA Ops:
  0.6 0.0 copy-start
  0.6 0.0 copy-start.1
  0.7 1.0 %copy-done.1 = bf16[32,5184]{1,0:T(8,128)(2,1)S(1)} copy-done((bf16[32,5184]{1,0:T(8,128)(2,1)S(1)}, bf16[32,5184]{1,0:T(8,128)(2,1)}, u32[]{:S(2)}) %copy-start.1) | copy-done | bytes 331800
  1.7 0.0 copy-start.2
  1.7 0.9 %copy-done.2 = bf16[32,8,512]{2,1,0:T(8,128)(2,1)S(1)} copy-done((bf16[32,8,512]{2,1,0:T(8,128)(2,1)S(1)}, bf16[32,8,512]{2,1,0:T(8,128)(2,1)}, u32[]{:S(2)}) %copy-start.2) | copy-done | bytes 262168
  2.6 0.0 copy-start.3
  2.6 0.7 %copy-done.3 = s32[8,512]{1,0:T(8,128)S(1)} copy-done((s32[8,512]{1,0:T(8,128)S(1)}, s32[8,512]{1,0:T(8,128)}, u32[]{:S(2)}) %copy-start.3) | copy-done | bytes 16408
  3.3 4.8 %shard_map.76 = (f32[8,2,32,512]{3,2,1,0:T(8,128)S(1)}, f32[8,2,32,512]{3,2,1,0:T(8,128)S(1)}, bf16[288,576]{1,0:T(8,128)(2,1)S(1)}, bf16[8,32,512]{2,1,0:T(8,128)(2,1)S(1)}, bf16[2,512]{1,0:T(2,128)(2,1)S(1)}) custom-call(bf16[32,8,512]{2,1,0:T(8,128)(2,1)S(1)} %copy-done.2, bf16[32,5184]{1,0:T(8,128)(2,1)S(1)} %copy-done.1, s32[8,512]{1,0:T(8,128)S(1)} %copy-done.3), custom_call_target="tpu_custom_call" | custom-call | flops 1358954496 | bytes 3145728 | tf_op jit(solution)/shard_map/pallas_call | solution.py:228
  8.1 0.1 convert_element_type.24
  8.2 0.1 collective-permute-start
  8.4 0.0 copy-done
  8.4 0.1 constant_dynamic-slice_fusion
  8.5 1.8 %collective-permute-done = f16[8,2,32,512]{3,2,1,0:T(8,128)(2,1)S(1)} collective-permute-done((f16[8,2,32,512]{3,2,1,0:T(8,128)(2,1)S(1)}, f16[8,2,32,512]{3,2,1,0:T(8,128)(2,1)S(1)}, u32[]{:S(2)}, u32[]{:S(2)}) %collective-permute-start) | collective-permute-done | bytes 524320 | tf_op jit(solution)/shard_map/ppermute | solution.py:255
  10.2 0.2 add_convert_fusion
  10.4 16.5 %all_to_all.15 = f16[8,2,32,512]{3,2,1,0:T(8,128)(2,1)S(1)} all-to-all(f16[8,2,32,512]{3,2,1,0:T(8,128)(2,1)S(1)} %add_convert_fusion), channel_id=1, replica_groups={{0,2,4,6,8,10,12,14},{1,3,5,7,9,11,13,15},{16,18,20,22,24,26,28,30},{17..., dimensions={0} | all-to-all | bytes 1048576 | tf_op jit(solution)/shard_map/all_to_all | solution.py:223
  26.9 0.1 convert_reduce_fusion
  27.0 4.4 %collective-permute-start.1 = (f32[2,32,512]{2,1,0:T(8,128)S(1)}, f32[2,32,512]{2,1,0:T(8,128)S(1)}, u32[]{:S(2)}, u32[]{:S(2)}) collective-permute-start(f32[2,32,512]{2,1,0:T(8,128)S(1)} %pad_maximum_fusion.1), channel_id=1, source_target_pairs={{0,120},{1,121},{2,122},{3,123},{4,124},{5,125},{6,126},{7,127},{8... | collective-permute-start | bytes 393224 | tf_op jit(solution)/shard_map/ppermute | solution.py:261
  31.4 4.0 %collective-permute-done.1 = f32[2,32,512]{2,1,0:T(8,128)S(1)} collective-permute-done((f32[2,32,512]{2,1,0:T(8,128)S(1)}, f32[2,32,512]{2,1,0:T(8,128)S(1)}, u32[]{:S(2)}, u32[]{:S(2)}) %collective-permute-start.1) | collective-permute-done | bytes 131104 | tf_op jit(solution)/shard_map/ppermute | solution.py:261
  35.5 11.0 %all_to_all.16.mine_ref.half_ref = bf16[8,2,32,512]{3,2,1,0:T(8,128)(2,1)S(1)} all-to-all(bf16[8,2,32,512]{3,2,1,0:T(8,128)(2,1)S(1)} %broadcast_in_dim.10), channel_id=1, replica_groups={{0,2,4,6,8,10,12,14},{1,3,5,7,9,11,13,15},{16,18,20,22,24,26,28,30},{17..., dimensions={0} | all-to-all | bytes 1048576 | tf_op jit(solution)/shard_map/all_to_all | solution.py:223
  46.6 0.0 collective-permute-start.2
  46.6 1.7 %shard_map.78 = f32[4,72,384]{2,1,0:T(8,128)S(1)} custom-call(bf16[8,2,32,512]{3,2,1,0:T(8,128)(2,1)S(1)} %all_to_all.16.mine_ref.half_ref, bf16[2,512]{1,0:T(2,128)(2,1)S(1)} %get-tuple-element.17.edge_ref, bf16[8,32,512]{2,1,0:T(8,128)(2,1)S(1)} %get-tuple-element.18.coef_ref), custom_call_target="tpu_custom_call" | custom-call | flops 679477248 | bytes 3145728 | tf_op jit(solution)/shard_map/pallas_call | solution.py:280
  48.2 0.2 collective-permute-done.2.other_ref.half_ref
  48.5 1.7 %shard_map.79 = f32[4,72,384]{2,1,0:T(8,128)S(1)} custom-call(bf16[8,2,32,512]{3,2,1,0:T(8,128)(2,1)S(1)} %collective-permute-done.2.other_ref.half_ref, bf16[2,512]{1,0:T(2,128)(2,1)S(1)} %get-tuple-element.17.edge_ref, bf16[8,32,512]{2,1,0:T(8,128)(2,1)S(1)} %get-tuple-element.18.coef_ref), custom_call_target="tpu_custom_call" | custom-call | flops 679477248 | bytes 3145728 | tf_op jit(solution)/shard_map/pallas_call | solution.py:281
  50.1 0.1 select_convert_fusion.1
  50.2 0.9 %pad_maximum_fusion = f16[8,72,384]{2,1,0:T(8,128)(2,1)} fusion(f16[4,72,384]{2,1,0:T(8,128)(2,1)S(1)} %get-tuple-element.27, f16[4,72,384]{2,1,0:T(8,128)(2,1)S(1)} %get-tuple-element.26), kind=kLoop, calls=%fused_computation.3 | loop fusion | flops 221184 | bytes 884736 | tf_op jit(solution)/shard_map/concatenate | solution.py:283
  51.1 0.0 copy-start.4
  51.1 6.8 %all-to-all-start.2 = ((f16[8,72,384]{2,1,0:T(8,128)(2,1)}), f16[8,72,384]{2,1,0:T(8,128)(2,1)S(1)}, u32[]{:S(2)}, u32[]{:S(2)}) async-start(f16[8,72,384]{2,1,0:T(8,128)(2,1)} %pad_maximum_fusion), calls=%async_computation.2 | async-start | bytes 884736 | tf_op jit(solution)/shard_map/all_to_all | solution.py:286
  57.9 0.0 copy-done.4
  57.9 0.1 copy.10.shrink_ref
  57.9 4.3 %shard_map.77 = (bf16[32,8,512]{2,1,0:T(8,128)(2,1)}, bf16[64,8,512]{2,1,0:T(8,128)(2,1)}) custom-call(bf16[8,2,32,512]{3,2,1,0:T(8,128)(2,1)S(1)} %all_to_all.16.mine_ref.half_ref, bf16[8,2,32,512]{3,2,1,0:T(8,128)(2,1)S(1)} %collective-permute-done.2.other_ref.half_ref, bf16[2,512]{1,0:T(2,128)(2,1)S(1)} %get-tuple-element.17.edge_ref, ...), custom_call_target="tpu_custom_call" | custom-call | flops 1358954496 | bytes 3145728 | tf_op jit(solution)/shard_map/pallas_call | solution.py:287
  62.3 6.7 %all-to-all-done.2 = f16[8,72,384]{2,1,0:T(8,128)(2,1)S(1)} async-done(((f16[8,72,384]{2,1,0:T(8,128)(2,1)}), f16[8,72,384]{2,1,0:T(8,128)(2,1)S(1)}, u32[]{:S(2)}, u32[]{:S(2)}) %all-to-all-start.2) | async-done | bytes 442400 | tf_op jit(solution)/shard_map/all_to_all | solution.py:286
  69.0 0.1 convert_reduce_fusion.1
  69.1 0.1 reshape.29
  69.2 0.2 copy.11
  69.5 0.8 %copy.12 = f32[32,648]{1,0:T(8,128)} copy(f32[32,648]{0,1:T(8,128)S(1)} %reshape.30) | data formatting | bytes 165888
  (10 shorter events, 0.2 us)
Async XLA Ops:
  0.6 7.7 %copy-start = (bf16[64,8,512]{2,1,0:T(8,128)(2,1)S(1)}, bf16[64,8,512]{2,1,0:T(8,128)(2,1)}, u32[]{:S(2)}) copy-start(bf16[64,8,512]{2,1,0:T(8,128)(2,1)} %param.5) | copy-start | bytes 1572868
  0.6 1.0 %copy-start.1 = (bf16[32,5184]{1,0:T(8,128)(2,1)S(1)}, bf16[32,5184]{1,0:T(8,128)(2,1)}, u32[]{:S(2)}) copy-start(bf16[32,5184]{1,0:T(8,128)(2,1)} %d_hbm.1) | copy-start | bytes 995332
  1.7 0.9 %copy-start.2 = (bf16[32,8,512]{2,1,0:T(8,128)(2,1)S(1)}, bf16[32,8,512]{2,1,0:T(8,128)(2,1)}, u32[]{:S(2)}) copy-start(bf16[32,8,512]{2,1,0:T(8,128)(2,1)} %coef_hbm.1) | copy-start | bytes 786436
  2.6 0.7 %copy-start.3 = (s32[8,512]{1,0:T(8,128)S(1)}, s32[8,512]{1,0:T(8,128)}, u32[]{:S(2)}) copy-start(s32[8,512]{1,0:T(8,128)} %seam_hbm.1) | copy-start | bytes 49156
  8.2 2.0 %collective-permute-start = (f16[8,2,32,512]{3,2,1,0:T(8,128)(2,1)S(1)}, f16[8,2,32,512]{3,2,1,0:T(8,128)(2,1)S(1)}, u32[]{:S(2)}, u32[]{:S(2)}) collective-permute-start(f16[8,2,32,512]{3,2,1,0:T(8,128)(2,1)S(1)} %convert_element_type.24), channel_id=1, source_target_pairs={{0,1},{1,0},{2,3},{3,2},{4,5},{5,4},{6,7},{7,6},{8,9},{9,8},{10,11... | collective-permute-start | bytes 1572872 | tf_op jit(solution)/shard_map/ppermute | solution.py:255
  27.0 8.4 %collective-permute-start.1 = (f32[2,32,512]{2,1,0:T(8,128)S(1)}, f32[2,32,512]{2,1,0:T(8,128)S(1)}, u32[]{:S(2)}, u32[]{:S(2)}) collective-permute-start(f32[2,32,512]{2,1,0:T(8,128)S(1)} %pad_maximum_fusion.1), channel_id=1, source_target_pairs={{0,120},{1,121},{2,122},{3,123},{4,124},{5,125},{6,126},{7,127},{8... | collective-permute-start | bytes 393224 | tf_op jit(solution)/shard_map/ppermute | solution.py:261
  46.6 1.9 %collective-permute-start.2 = (bf16[8,2,32,512]{3,2,1,0:T(8,128)(2,1)S(1)}, bf16[8,2,32,512]{3,2,1,0:T(8,128)(2,1)S(1)}, u32[]{:S(2)}, u32[]{:S(2)}) collective-permute-start(bf16[8,2,32,512]{3,2,1,0:T(8,128)(2,1)S(1)} %all_to_all.16.mine_ref.half_ref), channel_id=1, source_target_pairs={{0,1},{1,0},{2,3},{3,2},{4,5},{5,4},{6,7},{7,6},{8,9},{9,8},{10,11... | collective-permute-start | bytes 1572872 | tf_op jit(solution)/shard_map/ppermute | solution.py:264
  51.1 6.8 %copy-start.4 = (f32[32]{0:T(128)S(1)}, f32[32]{0:T(128)}, u32[]{:S(2)}) copy-start(f32[32]{0:T(128)} %param.8) | copy-start | bytes 388
  51.1 17.9 %all-to-all-start.2 = ((f16[8,72,384]{2,1,0:T(8,128)(2,1)}), f16[8,72,384]{2,1,0:T(8,128)(2,1)S(1)}, u32[]{:S(2)}, u32[]{:S(2)}) async-start(f16[8,72,384]{2,1,0:T(8,128)(2,1)} %pad_maximum_fusion), calls=%async_computation.2 | async-start | bytes 884736 | tf_op jit(solution)/shard_map/all_to_all | solution.py:286

commit v3 on v2

--- a/solution.py
+++ b/solution.py
@@ -38,21 +38,8 @@
     return wide[:, LEFT + j : LEFT + j + TILE_W]
 
 
-def synthesis_kernel(
-    coef_hbm, d_hbm, seam_hbm,
-    keep_ref, send_ref, acorr_ref, rows_ref, edge_ref,
-    coef_ref, d_ref, seam_ref, by_band, by_atom, turned, asynth, cols, acc, sems,
-):
-    atoms = coef_ref.shape[0]
-    copies = [
-        pltpu.make_async_copy(source, target, sems.at[i])
-        for i, (source, target) in enumerate(
-            ((d_hbm, d_ref), (coef_hbm, coef_ref), (seam_hbm, seam_ref))
-        )
-    ]
-    for copy in copies:
-        copy.start()
-    copies[0].wait()
+def atoms_kernel(d_ref, acorr_ref, asynth_ref, by_band, by_atom, turned):
+    atoms = d_ref.shape[0]
     d = d_ref[...].astype(jnp.float32)
     for c in range(C):
         by_band[c * atoms : (c + 1) * atoms, 0:TAPS] = d[:, c * TAPS : (c + 1) * TAPS]
@@ -64,24 +51,23 @@
         block = by_atom[pl.ds(tap, atoms, stride=TAP_ROWS), :][:, 0:C]
         acorr_ref[dy * atoms : (dy + 1) * atoms, dx * C : (dx + 1) * C] = block.astype(jnp.bfloat16)
         turned[dx * atoms : (dx + 1) * atoms, dy * C : (dy + 1) * C] = block
-    asynth[...] = jnp.transpose(turned[...]).astype(jnp.bfloat16)
-
-    copies[1].wait()
-    copies[2].wait()
-    position = lax.axis_index("tile")
-    strips = seam_ref.shape[0]
-    w_up = seam_weight(seam_ref, lax.rem(position + (strips - 1), strips))
-    w_down = seam_weight(seam_ref, position)
-    edge_ref[0:1, :] = w_up
-    edge_ref[1:2, :] = w_down
-    rows_ref[...] = turn(coef_ref[...])
+    bands = jnp.transpose(turned[...]).astype(jnp.bfloat16)
+    for dy in range(TAP):
+        for half in range(2):
+            asynth_ref[half, dy * HALF : (dy + 1) * HALF, :] = bands[
+                dy * C + half * HALF : dy * C + (half + 1) * HALF, :
+            ]
+
+
+def synthesize(a, rows_ref, w_up, w_down, out_ref, cols, acc):
+    atoms = rows_ref.shape[1]
     acc[...] = jnp.zeros_like(acc)
 
     def add(slot, q, low, high):
         dy = low - (ROWS - 1) + q
         count = high - low + 1
-        acc[low * C : (high + 1) * C, :] += jnp.dot(
-            asynth[dy * C : (dy + count) * C, :], cols[slot], preferred_element_type=jnp.float32
+        acc[low * HALF : (high + 1) * HALF, :] += jnp.dot(
+            a[dy * HALF : (dy + count) * HALF, :], cols[slot], preferred_element_type=jnp.float32
         )
 
     for q in range(ROWS):
@@ -96,14 +82,27 @@
             add(1, q, HALO + ROWS, high)
         else:
             add(1, q, low, HALO - 1)
-    core = lax.rem(lax.axis_index("atom"), 2)
-    mine = pl.multiple_of(core * HALF, HALF)
-    other = pl.multiple_of((1 - core) * HALF, HALF)
     for j in range(ROWS):
         edge = HALO + ROWS + (HALO - 1) - j if j < HALO else ROWS - 1 - j
         for part, at in ((0, HALO + ROWS - 1 - j), (1, edge)):
-            keep_ref[j, part] = acc[pl.ds(at * C + mine, HALF), :]
-            send_ref[j, part] = acc[pl.ds(at * C + other, HALF), :].astype(send_ref.dtype)
+            out_ref[j, part] = acc[at * HALF : (at + 1) * HALF, :]
+
+
+def send_kernel(coef_ref, a_ref, seam_ref, send_ref, rows_ref, edge_ref, cols, acc):
+    position = lax.axis_index("tile")
+    strips = seam_ref.shape[0]
+    w_up = seam_weight(seam_ref, lax.rem(position + (strips - 1), strips))
+    w_down = seam_weight(seam_ref, position)
+    edge_ref[0:1, :] = w_up
+    edge_ref[1:2, :] = w_down
+    rows_ref[...] = turn(coef_ref[...])
+    a = a_ref[1 - lax.rem(lax.axis_index("atom"), 2)]
+    synthesize(a, rows_ref, w_up, w_down, send_ref, cols, acc)
+
+
+def keep_kernel(rows_ref, a_ref, edge_ref, keep_ref, cols, acc):
+    a = a_ref[lax.rem(lax.axis_index("atom"), 2)]
+    synthesize(a, rows_ref, edge_ref[0:1, :], edge_ref[1:2, :], keep_ref, cols, acc)
 
 
 def pad_row(core, mine_ref, other_ref, w_up, w_down, r):
@@ -198,7 +197,6 @@
 
 
 VMEM = pl.BlockSpec(memory_space=pltpu.VMEM)
-HBM = pl.BlockSpec(memory_space=pltpu.HBM)
 
 
 def per_device(image, coeffs, dictionary, shrink, seam_map):
@@ -225,32 +223,50 @@
     params = pltpu.CompilerParams(vmem_limit_bytes=48 * 1024 * 1024)
     flops = 2 * 72 * atoms * C * TAP * TILE_W
     cost = pl.CostEstimate(flops=flops, bytes_accessed=3 << 20, transcendentals=0)
-    keep, send, a_corr, coef_rows, edges = pl.pallas_call(
-        synthesis_kernel,
+    a_corr, a_synth = pl.pallas_call(
+        atoms_kernel,
         out_shape=(
-            jax.ShapeDtypeStruct((ROWS, 2, HALF, TILE_W), jnp.float32),
-            jax.ShapeDtypeStruct((ROWS, 2, HALF, TILE_W), jnp.float32),
             jax.ShapeDtypeStruct((TAP * atoms, TAP * C), jnp.bfloat16),
+            jax.ShapeDtypeStruct((2, TAP * HALF, TAP * atoms), jnp.bfloat16),
+        ),
+        in_specs=[VMEM],
+        out_specs=(VMEM,) * 2,
+        scratch_shapes=[
+            pltpu.VMEM((C * atoms, 128), jnp.float32),
+            pltpu.VMEM((atoms * TAP_ROWS, 128), jnp.float32),
+            pltpu.VMEM((TAP * atoms, TAP * C), jnp.float32),
+        ],
+        compiler_params=params,
+        cost_estimate=cost,
+    )(dictionary)
+    sums = jax.ShapeDtypeStruct((ROWS, 2, HALF, TILE_W), jnp.float32)
+    room = [
+        pltpu.VMEM((2, TAP * atoms, TILE_W), jnp.bfloat16),
+        pltpu.VMEM((2 * ROWS * HALF, TILE_W), jnp.float32),
+    ]
+    half_cost = pl.CostEstimate(flops=flops // 2, bytes_accessed=3 << 20, transcendentals=0)
+    send, coef_rows, edges = pl.pallas_call(
+        send_kernel,
+        out_shape=(
+            sums,
             jax.ShapeDtypeStruct((ROWS, atoms, TILE_W), jnp.bfloat16),
             jax.ShapeDtypeStruct((2, TILE_W), jnp.bfloat16),
         ),
-        in_specs=[HBM] * 3,
-        out_specs=(VMEM,) * 5,
-        scratch_shapes=[
-            pltpu.VMEM(coeffs.shape, jnp.bfloat16),
-            pltpu.VMEM(dictionary.shape, jnp.bfloat16),
-            pltpu.VMEM(seam_map.shape, jnp.int32),
-            pltpu.VMEM((C * atoms, 128), jnp.float32),
-            pltpu.VMEM((atoms * TAP_ROWS, 128), jnp.float32),
-            pltpu.VMEM((TAP * atoms, TAP * C), jnp.float32),
-            pltpu.VMEM((TAP * C, TAP * atoms), jnp.bfloat16),
-            pltpu.VMEM((2, TAP * atoms, TILE_W), jnp.bfloat16),
-            pltpu.VMEM((2 * ROWS * C, TILE_W), jnp.float32),
-            pltpu.SemaphoreType.DMA((3,)),
-        ],
-        compiler_params=params,
-        cost_estimate=cost,
-    )(coeffs, dictionary, seam_map)
+        in_specs=[VMEM] * 3,
+        out_specs=(VMEM,) * 3,
+        scratch_shapes=room,
+        compiler_params=params,
+        cost_estimate=half_cost,
+    )(coeffs, a_synth, seam_map)
+    keep = pl.pallas_call(
+        keep_kernel,
+        out_shape=sums,
+        in_specs=[VMEM] * 3,
+        out_specs=VMEM,
+        scratch_shapes=room,
+        compiler_params=params,
+        cost_estimate=half_cost,
+    )(coef_rows, a_synth, edges)
     image_row = lax.dynamic_slice(image, (core * HALF, member, 0), (HALF, 1, TILE_W))[:, 0]
     other = lax.ppermute(send.astype(jnp.float16), "atom", swap)
     partial = (keep + other.astype(jnp.float32)).astype(jnp.float16)
@@ -275,7 +291,7 @@
             pltpu.VMEM((2, ROWS * atoms, ROWS * TILE_W), jnp.bfloat16),
         ],
         compiler_params=params,
-        cost_estimate=pl.CostEstimate(flops=flops // 2, bytes_accessed=3 << 20, transcendentals=0),
+        cost_estimate=half_cost,
     )
     my_terms = term_half(mine, edges, coef_rows)
     their_terms = term_half(theirs, edges, coef_rows)

time: 70.6 us -> 69.2 us (0.980)
  waiting for transfers between devices: 12.7 us -> 10.8 us
  local copies, waits for them, and re-layouts: 4.08 us -> 2.42 us
  blocking collectives: 27.5 us -> 28.4 us
  starting transfers between devices: 11.3 us -> 12.1 us
    ppermute x1, waiting for transfers between devices: 1.76 us -> 0.01 us  [per_device(): other = lax.ppermute(send.astype(jnp.float16), 'atom', swap)]
    unnamed x12, local copies, waits for them, and re-layouts: 3.5 us -> 1.84 us
    all_to_all x2, blocking collectives: 27.5 us -> 28.4 us  [exchange(): lax.all_to_all(field, 'atom', 0, 0, tiled=True, axis_index_groups=chips)]
    pallas_call x1 -> x3, Pallas kernels: 4.78 us -> 5.26 us  [the longest x1 1.95 us: per_device(): pl.pallas_call(send_kernel, out_shape=(sums, jax.ShapeDtypeStruct((ROWS,...]
  transfers between devices with their start and end apart: 4 -> 4, of which waited for: 4 -> 3; matrix products, arithmetic and copies ran while one was open for 0% -> 0% of each run, Pallas kernels for 8% -> 11%
where the time goes in v3:
time: 69.2 us; the launch traced here: 68.9 us
  blocking collectives  28.4 us (41%)
  Pallas kernels  12.9 us (19%)
  starting transfers between devices  12.1 us (17%)
  waiting for transfers between devices  10.8 us (16%)
  local copies, waits for them, and re-layouts  2.42 us (3%)
  other arithmetic  1.46 us (2%)
  between operations  0.88 us (1%)
    all_to_all x2, blocking collectives, exchange(): lax.all_to_all(field, 'atom', 0, 0, tiled=True, axis_index_groups=chips)  28.4 us
    all_to_all x1, starting transfers between devices, per_device(): got = lax.all_to_all(terms, 'tile', 0, 0, tiled=True)  7.46 us
    all_to_all x1, waiting for transfers between devices, per_device(): got = lax.all_to_all(terms, 'tile', 0, 0, tiled=True)  6.73 us
    ppermute x1, starting transfers between devices, per_device(): facing = lax.ppermute(held, ('tile', 'atom'), pairs)  4.56 us
    pallas_call x1, Pallas kernels, per_device(): pl.pallas_call(coeffs_kernel, out_shape=(jax.ShapeDtypeStruct((atoms, ROW...  4.32 us
    ppermute x1, waiting for transfers between devices, per_device(): facing = lax.ppermute(held, ('tile', 'atom'), pairs)  3.81 us
    pallas_call x1, Pallas kernels, per_device(): pl.pallas_call(send_kernel, out_shape=(sums, jax.ShapeDtypeStruct((ROWS,...  1.95 us
    unnamed x12, local copies, waits for them, and re-layouts  1.84 us
  transfers between devices with their start and end apart: 4, of which 3 were waited for; matrix products, arithmetic and copies ran while one was open for 0% of the time, Pallas kernels for 11%

profile of v3, /device:TPU:0, one launch (start us, length us, event | category | flops | bytes accessed | tf_op | source)
XLA Modules:
  0.0 68.9 jit_solution(10638146183483335777)
XLA Ops:
  0.6 0.0 copy-start
  0.6 0.0 copy-start.1
  0.7 1.0 %copy-done.1 = bf16[32,5184]{1,0:T(8,128)(2,1)S(1)} copy-done((bf16[32,5184]{1,0:T(8,128)(2,1)S(1)}, bf16[32,5184]{1,0:T(8,128)(2,1)}, u32[]{:S(2)}) %copy-start.1) | copy-done | bytes 331800
  1.7 0.0 copy-start.2
  1.7 0.0 copy-start.3
  1.7 1.5 %shard_map.76 = (bf16[288,576]{1,0:T(8,128)(2,1)S(1)}, bf16[2,288,288]{2,1,0:T(8,128)(2,1)S(1)}) custom-call(bf16[32,5184]{1,0:T(8,128)(2,1)S(1)} %copy-done.1), custom_call_target="tpu_custom_call" | custom-call | flops 1358954496 | bytes 3145728 | tf_op jit(solution)/shard_map/pallas_call | solution.py:226
  3.2 0.0 copy-done.2
  3.2 0.0 copy-done.3
  3.2 2.0 %shard_map.77 = (f32[8,2,32,512]{3,2,1,0:T(8,128)S(1)}, bf16[8,32,512]{2,1,0:T(8,128)(2,1)S(1)}, bf16[2,512]{1,0:T(2,128)(2,1)S(1)}) custom-call(bf16[32,8,512]{2,1,0:T(8,128)(2,1)S(1)} %copy-done.2, bf16[2,288,288]{2,1,0:T(8,128)(2,1)S(1)} %get-tuple-element.13.a_ref, s32[8,512]{1,0:T(8,128)S(1)} %copy-done.3), custom_call_target="tpu_custom_call" | custom-call | flops 679477248 | bytes 3145728 | tf_op jit(solution)/shard_map/pallas_call | solution.py:248
  5.1 0.1 convert_element_type.24
  5.3 0.1 collective-permute-start
  5.4 0.0 copy-done
  5.4 0.1 constant_dynamic-slice_fusion
  5.5 1.8 %shard_map.78 = f32[8,2,32,512]{3,2,1,0:T(8,128)S(1)} custom-call(bf16[8,32,512]{2,1,0:T(8,128)(2,1)S(1)} %get-tuple-element.14.rows_ref.coef_ref, bf16[2,288,288]{2,1,0:T(8,128)(2,1)S(1)} %get-tuple-element.13.a_ref, bf16[2,512]{1,0:T(2,128)(2,1)S(1)} %get-tuple-element.15.edge_ref), custom_call_target="tpu_custom_call" | custom-call | flops 679477248 | bytes 3145728 | tf_op jit(solution)/shard_map/pallas_call | solution.py:261
  7.3 0.0 collective-permute-done
  7.3 0.2 add_convert_fusion
  7.5 16.7 %all_to_all.15 = f16[8,2,32,512]{3,2,1,0:T(8,128)(2,1)S(1)} all-to-all(f16[8,2,32,512]{3,2,1,0:T(8,128)(2,1)S(1)} %add_convert_fusion), channel_id=1, replica_groups={{0,2,4,6,8,10,12,14},{1,3,5,7,9,11,13,15},{16,18,20,22,24,26,28,30},{17..., dimensions={0} | all-to-all | bytes 1048576 | tf_op jit(solution)/shard_map/all_to_all | solution.py:221
  24.2 0.1 convert_reduce_fusion
  24.3 4.6 %collective-permute-start.1 = (f32[2,32,512]{2,1,0:T(8,128)S(1)}, f32[2,32,512]{2,1,0:T(8,128)S(1)}, u32[]{:S(2)}, u32[]{:S(2)}) collective-permute-start(f32[2,32,512]{2,1,0:T(8,128)S(1)} %pad_maximum_fusion.1), channel_id=1, source_target_pairs={{0,120},{1,121},{2,122},{3,123},{4,124},{5,125},{6,126},{7,127},{8... | collective-permute-start | bytes 393224 | tf_op jit(solution)/shard_map/ppermute | solution.py:277
  28.9 3.8 %collective-permute-done.1 = f32[2,32,512]{2,1,0:T(8,128)S(1)} collective-permute-done((f32[2,32,512]{2,1,0:T(8,128)S(1)}, f32[2,32,512]{2,1,0:T(8,128)S(1)}, u32[]{:S(2)}, u32[]{:S(2)}) %collective-permute-start.1) | collective-permute-done | bytes 131104 | tf_op jit(solution)/shard_map/ppermute | solution.py:277
  32.8 11.7 %all_to_all.16.mine_ref.half_ref = bf16[8,2,32,512]{3,2,1,0:T(8,128)(2,1)S(1)} all-to-all(bf16[8,2,32,512]{3,2,1,0:T(8,128)(2,1)S(1)} %broadcast_in_dim.10), channel_id=1, replica_groups={{0,2,4,6,8,10,12,14},{1,3,5,7,9,11,13,15},{16,18,20,22,24,26,28,30},{17..., dimensions={0} | all-to-all | bytes 1048576 | tf_op jit(solution)/shard_map/all_to_all | solution.py:221
  44.5 0.0 collective-permute-start.2
  44.5 1.7 %shard_map.80 = f32[4,72,384]{2,1,0:T(8,128)S(1)} custom-call(bf16[8,2,32,512]{3,2,1,0:T(8,128)(2,1)S(1)} %all_to_all.16.mine_ref.half_ref, bf16[2,512]{1,0:T(2,128)(2,1)S(1)} %get-tuple-element.15.edge_ref, bf16[8,32,512]{2,1,0:T(8,128)(2,1)S(1)} %get-tuple-element.14.rows_ref.coef_ref), custom_call_target="tpu_custom_call" | custom-call | flops 679477248 | bytes 3145728 | tf_op jit(solution)/shard_map/pallas_call | solution.py:296
  46.2 0.2 collective-permute-done.2.other_ref.half_ref
  46.4 1.7 %shard_map.81 = f32[4,72,384]{2,1,0:T(8,128)S(1)} custom-call(bf16[8,2,32,512]{3,2,1,0:T(8,128)(2,1)S(1)} %collective-permute-done.2.other_ref.half_ref, bf16[2,512]{1,0:T(2,128)(2,1)S(1)} %get-tuple-element.15.edge_ref, bf16[8,32,512]{2,1,0:T(8,128)(2,1)S(1)} %get-tuple-element.14.rows_ref.coef_ref), custom_call_target="tpu_custom_call" | custom-call | flops 679477248 | bytes 3145728 | tf_op jit(solution)/shard_map/pallas_call | solution.py:297
  48.1 0.1 select_convert_fusion.1
  48.2 0.9 %pad_maximum_fusion = f16[8,72,384]{2,1,0:T(8,128)(2,1)} fusion(f16[4,72,384]{2,1,0:T(8,128)(2,1)S(1)} %get-tuple-element.27, f16[4,72,384]{2,1,0:T(8,128)(2,1)S(1)} %get-tuple-element.26), kind=kLoop, calls=%fused_computation.3 | loop fusion | flops 221184 | bytes 884736 | tf_op jit(solution)/shard_map/concatenate | solution.py:299
  49.1 0.0 copy-start.4
  49.1 7.5 %all-to-all-start.2 = ((f16[8,72,384]{2,1,0:T(8,128)(2,1)}), f16[8,72,384]{2,1,0:T(8,128)(2,1)S(1)}, u32[]{:S(2)}, u32[]{:S(2)}) async-start(f16[8,72,384]{2,1,0:T(8,128)(2,1)} %pad_maximum_fusion), calls=%async_computation.2 | async-start | bytes 884736 | tf_op jit(solution)/shard_map/all_to_all | solution.py:302
  56.5 0.0 copy-done.4
  56.5 0.1 copy.10.shrink_ref
  56.6 4.3 %shard_map.79 = (bf16[32,8,512]{2,1,0:T(8,128)(2,1)}, bf16[64,8,512]{2,1,0:T(8,128)(2,1)}) custom-call(bf16[8,2,32,512]{3,2,1,0:T(8,128)(2,1)S(1)} %all_to_all.16.mine_ref.half_ref, bf16[8,2,32,512]{3,2,1,0:T(8,128)(2,1)S(1)} %collective-permute-done.2.other_ref.half_ref, bf16[2,512]{1,0:T(2,128)(2,1)S(1)} %get-tuple-element.15.edge_ref, ...), custom_call_target="tpu_custom_call" | custom-call | flops 1358954496 | bytes 3145728 | tf_op jit(solution)/shard_map/pallas_call | solution.py:303
  60.9 6.7 %all-to-all-done.2 = f16[8,72,384]{2,1,0:T(8,128)(2,1)S(1)} async-done(((f16[8,72,384]{2,1,0:T(8,128)(2,1)}), f16[8,72,384]{2,1,0:T(8,128)(2,1)S(1)}, u32[]{:S(2)}, u32[]{:S(2)}) %all-to-all-start.2) | async-done | bytes 442400 | tf_op jit(solution)/shard_map/all_to_all | solution.py:302
  67.7 0.1 convert_reduce_fusion.1
  67.8 0.1 reshape.29
  67.9 0.2 copy.11
  68.1 0.8 %copy.12 = f32[32,648]{1,0:T(8,128)} copy(f32[32,648]{0,1:T(8,128)S(1)} %reshape.30) | data formatting | bytes 165888
  (10 shorter events, 0.2 us)
Async XLA Ops:
  0.6 4.8 %copy-start = (bf16[64,8,512]{2,1,0:T(8,128)(2,1)S(1)}, bf16[64,8,512]{2,1,0:T(8,128)(2,1)}, u32[]{:S(2)}) copy-start(bf16[64,8,512]{2,1,0:T(8,128)(2,1)} %param.5) | copy-start | bytes 1572868
  0.6 1.0 %copy-start.1 = (bf16[32,5184]{1,0:T(8,128)(2,1)S(1)}, bf16[32,5184]{1,0:T(8,128)(2,1)}, u32[]{:S(2)}) copy-start(bf16[32,5184]{1,0:T(8,128)(2,1)} %d_ref.1) | copy-start | bytes 995332
  1.7 1.5 %copy-start.2 = (bf16[32,8,512]{2,1,0:T(8,128)(2,1)S(1)}, bf16[32,8,512]{2,1,0:T(8,128)(2,1)}, u32[]{:S(2)}) copy-start(bf16[32,8,512]{2,1,0:T(8,128)(2,1)} %coef_ref.1) | copy-start | bytes 786436
  1.7 1.5 %copy-start.3 = (s32[8,512]{1,0:T(8,128)S(1)}, s32[8,512]{1,0:T(8,128)}, u32[]{:S(2)}) copy-start(s32[8,512]{1,0:T(8,128)} %seam_ref.1) | copy-start | bytes 49156
  5.3 2.1 %collective-permute-start = (f16[8,2,32,512]{3,2,1,0:T(8,128)(2,1)S(1)}, f16[8,2,32,512]{3,2,1,0:T(8,128)(2,1)S(1)}, u32[]{:S(2)}, u32[]{:S(2)}) collective-permute-start(f16[8,2,32,512]{3,2,1,0:T(8,128)(2,1)S(1)} %convert_element_type.24), channel_id=1, source_target_pairs={{0,1},{1,0},{2,3},{3,2},{4,5},{5,4},{6,7},{7,6},{8,9},{9,8},{10,11... | collective-permute-start | bytes 1572872 | tf_op jit(solution)/shard_map/ppermute | solution.py:271
  24.3 8.4 %collective-permute-start.1 = (f32[2,32,512]{2,1,0:T(8,128)S(1)}, f32[2,32,512]{2,1,0:T(8,128)S(1)}, u32[]{:S(2)}, u32[]{:S(2)}) collective-permute-start(f32[2,32,512]{2,1,0:T(8,128)S(1)} %pad_maximum_fusion.1), channel_id=1, source_target_pairs={{0,120},{1,121},{2,122},{3,123},{4,124},{5,125},{6,126},{7,127},{8... | collective-permute-start | bytes 393224 | tf_op jit(solution)/shard_map/ppermute | solution.py:277
  44.5 1.9 %collective-permute-start.2 = (bf16[8,2,32,512]{3,2,1,0:T(8,128)(2,1)S(1)}, bf16[8,2,32,512]{3,2,1,0:T(8,128)(2,1)S(1)}, u32[]{:S(2)}, u32[]{:S(2)}) collective-permute-start(bf16[8,2,32,512]{3,2,1,0:T(8,128)(2,1)S(1)} %all_to_all.16.mine_ref.half_ref), channel_id=1, source_target_pairs={{0,1},{1,0},{2,3},{3,2},{4,5},{5,4},{6,7},{7,6},{8,9},{9,8},{10,11... | collective-permute-start | bytes 1572872 | tf_op jit(solution)/shard_map/ppermute | solution.py:280
  49.1 7.5 %copy-start.4 = (f32[32]{0:T(128)S(1)}, f32[32]{0:T(128)}, u32[]{:S(2)}) copy-start(f32[32]{0:T(128)} %param.8) | copy-start | bytes 388
  49.1 18.6 %all-to-all-start.2 = ((f16[8,72,384]{2,1,0:T(8,128)(2,1)}), f16[8,72,384]{2,1,0:T(8,128)(2,1)S(1)}, u32[]{:S(2)}, u32[]{:S(2)}) async-start(f16[8,72,384]{2,1,0:T(8,128)(2,1)} %pad_maximum_fusion), calls=%async_computation.2 | async-start | bytes 884736 | tf_op jit(solution)/shard_map/all_to_all | solution.py:302

commit v4 on v3

--- a/solution.py
+++ b/solution.py
@@ -16,8 +16,8 @@
 HALF = C // 2
 ROWS = 8
 TAP_ROWS = 88
-LANES = 384
-SHRINK_TERMS = 2.0**-5
+LANES = 256
+SHRINK_TERMS = 2.0**-6
 
 step_size = 0.1
 eps_sq = 0.01
@@ -158,16 +158,18 @@
         )
     edge = jnp.zeros((TAP * HALF, atoms), jnp.float32)
     total = jnp.concatenate([edge, sums[0]], axis=1) + jnp.concatenate([sums[1], edge], axis=1)
-    total = jnp.concatenate(
-        [total * scale, jnp.zeros((TAP * HALF, LANES - TAP * atoms), jnp.float32)], axis=1
-    )
+    total = total * scale
     parts = term_ref.shape[0]
     per = HALF // parts
-    for dx in range(TAP):
-        for t in range(parts):
-            term_ref[t, dx * per : (dx + 1) * per, :] = total[
-                dx * HALF + t * per : dx * HALF + (t + 1) * per, :
-            ]
+    main = TAP * per
+    for t in range(parts):
+        blocks = [total[dx * HALF + t * per : dx * HALF + (t + 1) * per, :] for dx in range(TAP)]
+        for dx in range(TAP):
+            term_ref[t, dx * per : (dx + 1) * per, :] = blocks[dx][:, :LANES]
+        rest = [block[:, LANES:] for block in blocks]
+        term_ref[t, main : main + per, :] = jnp.concatenate(rest[:-1], axis=1)
+        gap = jnp.zeros((per, LANES - atoms), jnp.float32)
+        term_ref[t, main + per : main + 2 * per, :] = jnp.concatenate([rest[-1], gap], axis=1)
 
 
 def coeffs_kernel(
@@ -190,7 +192,7 @@
             a_ref[low * atoms : (high + 1) * atoms, :], cols[slot], preferred_element_type=jnp.float32
         )
     u = coef_ref[...].reshape(ROWS * atoms, TILE_W).astype(jnp.float32) + step_size * acc[...]
-    threshold = jnp.concatenate([shrink_ref[...]] * ROWS, axis=0)
+    threshold = jnp.concatenate([shrink_ref[:, 0:1]] * ROWS, axis=0)
     u = u - threshold * u / jnp.sqrt(u * u + eps_sq)
     new_ref[...] = turn(u.reshape(ROWS, atoms, TILE_W))
     resid_ref[...] = turn(own[...])
@@ -270,11 +272,14 @@
     image_row = lax.dynamic_slice(image, (core * HALF, member, 0), (HALF, 1, TILE_W))[:, 0]
     other = lax.ppermute(send.astype(jnp.float16), "atom", swap)
     partial = (keep + other.astype(jnp.float32)).astype(jnp.float16)
-    partial, image_row, threshold = lax.optimization_barrier((partial, image_row, shrink[:, None]))
+    partial, image_row = lax.optimization_barrier((partial, image_row))
     pieces = exchange(partial)
     total = jnp.sum(pieces.astype(jnp.float32), axis=0)
     held = jnp.stack([image_row.astype(jnp.float32) - total[0], total[1]])
+    held, shrink = lax.optimization_barrier((held, shrink))
     facing = lax.ppermute(held, ("tile", "atom"), pairs)
+    threshold = jnp.broadcast_to(shrink[:, None], (atoms, 128))
+    facing, threshold = lax.optimization_barrier((facing, threshold))
     rows_two = jnp.stack([held[0] - facing[1], facing[0] - held[1]]).astype(jnp.bfloat16)
     mine = exchange(jnp.broadcast_to(rows_two[None], (ROWS, 2, HALF, TILE_W)))
     theirs = lax.ppermute(mine, "atom", swap)
@@ -283,7 +288,7 @@
     per = C // strips
     term_half = pl.pallas_call(
         functools.partial(terms_kernel, scale=scale),
-        out_shape=jax.ShapeDtypeStruct((strips // 2, TAP * per, LANES), jnp.float32),
+        out_shape=jax.ShapeDtypeStruct((strips // 2, (TAP + 2) * per, LANES), jnp.float32),
         in_specs=[VMEM] * 3,
         out_specs=VMEM,
         scratch_shapes=[
@@ -296,10 +301,13 @@
     my_terms = term_half(mine, edges, coef_rows)
     their_terms = term_half(theirs, edges, coef_rows)
     first = core == 0
+    side = lax.axis_index("tile") % 2 == 0
     terms = jnp.concatenate(
         [jnp.where(first, my_terms, their_terms), jnp.where(first, their_terms, my_terms)]
-    ).astype(jnp.float16)
-    got = lax.all_to_all(terms, "tile", 0, 0, tiled=True)
+    ).reshape(strips // 2, 2, (TAP + 2) * per, LANES)
+    away = jnp.where(side, terms[:, 1], terms[:, 0]).astype(jnp.float16)
+    stay = jnp.where(side, terms[:, 0], terms[:, 1])
+    across = lax.ppermute(away, "tile", [(i, i ^ 1) for i in range(strips)])
     new_coeffs, residual = pl.pallas_call(
         coeffs_kernel,
         out_shape=(
@@ -316,8 +324,22 @@
         compiler_params=params,
         cost_estimate=cost,
     )(mine, theirs, edges, coef_rows, a_corr, threshold)
-    step = jnp.sum(got.astype(jnp.float32), axis=0)[:, : TAP * atoms] * (1.0 / SHRINK_TERMS)
-    step = step.reshape(TAP, per, TAP, atoms)
+    across, new_coeffs, residual = lax.optimization_barrier((across, new_coeffs, residual))
+    pair_terms = (stay + across.astype(jnp.float32)).astype(jnp.float16)
+    lines = strips // 2
+    line = lax.axis_index("tile") // 2
+    ahead = lax.dynamic_slice(
+        jnp.concatenate([pair_terms, pair_terms]), (line, 0, 0), (lines, (TAP + 2) * per, LANES)
+    )
+    got = [ahead[0]]
+    for hops in (2, 1, 3):
+        route = [(i, (i + 2 * hops) % strips) for i in range(strips)]
+        got.append(lax.ppermute(ahead[hops], "tile", route))
+    step = sum(piece.astype(jnp.float32) for piece in got) * (1.0 / SHRINK_TERMS)
+    main = step[: TAP * per].reshape(TAP, per, TAP - 1, atoms)
+    rest = step[TAP * per : (TAP + 1) * per].reshape(per, TAP - 1, atoms).transpose(1, 0, 2)
+    rest = jnp.concatenate([rest, step[None, (TAP + 1) * per :, :atoms]])
+    step = jnp.concatenate([main, rest[:, :, None, :]], axis=2)
     atom_step = step.transpose(3, 1, 2, 0).reshape(atoms, per * TAPS)
     return (new_coeffs, residual, atom_step)
 

time: 69.2 us -> 67.2 us (0.971)
  waiting for transfers between devices: 10.8 us -> 8.28 us
  starting transfers between devices: 12.1 us -> 12.9 us
    ppermute x0 -> x4, starting transfers between devices: none -> 8.3 us  [the longest x3 5.65 us: per_device(): got.append(lax.ppermute(ahead[hops], 'tile', route))]
    all_to_all x1 -> x0, starting transfers between devices: 7.46 us -> none  [per_device(): got = lax.all_to_all(terms, 'tile', 0, 0, tiled=True)]
    all_to_all x1 -> x0, waiting for transfers between devices: 6.73 us -> none  [per_device(): got = lax.all_to_all(terms, 'tile', 0, 0, tiled=True)]
    ppermute x0 -> x4, waiting for transfers between devices: none -> 4.28 us  [the longest x3 2.69 us: per_device(): got.append(lax.ppermute(ahead[hops], 'tile', route))]
    concatenate x1, other arithmetic: 0.87 us -> 0.05 us  [per_device(): jnp.concatenate([jnp.where(first, my_terms, their_terms), jnp.where(first...]
  transfers between devices with their start and end apart: 4 -> 7, of which waited for: 3 -> 6; matrix products, arithmetic and copies ran while one was open for 0% -> 0% of each run, Pallas kernels for 11% -> 12%
where the time goes in v4:
time: 67.2 us; the launch traced here: 66.9 us
  blocking collectives  28.4 us (42%)
  Pallas kernels  13 us (19%)
  starting transfers between devices  12.9 us (19%)
  waiting for transfers between devices  8.28 us (12%)
  local copies, waits for them, and re-layouts  2.49 us (4%)
  between operations  0.95 us (1%)
  other arithmetic  0.84 us (1%)
    all_to_all x2, blocking collectives, exchange(): lax.all_to_all(field, 'atom', 0, 0, tiled=True, axis_index_groups=chips)  28.4 us
    ppermute x3, starting transfers between devices, per_device(): got.append(lax.ppermute(ahead[hops], 'tile', route))  5.65 us
    ppermute x1, starting transfers between devices, per_device(): facing = lax.ppermute(held, ('tile', 'atom'), pairs)  4.56 us
    pallas_call x1, Pallas kernels, per_device(): pl.pallas_call(coeffs_kernel, out_shape=(jax.ShapeDtypeStruct((atoms, ROW...  4.31 us
    ppermute x1, waiting for transfers between devices, per_device(): facing = lax.ppermute(held, ('tile', 'atom'), pairs)  3.81 us
    ppermute x3, waiting for transfers between devices, per_device(): got.append(lax.ppermute(ahead[hops], 'tile', route))  2.69 us
    ppermute x1, starting transfers between devices, per_device(): across = lax.ppermute(away, 'tile', [(i, i ^ 1) for i in range(strips)])  2.65 us
    pallas_call x1, Pallas kernels, per_device(): pl.pallas_call(send_kernel, out_shape=(sums, jax.ShapeDtypeStruct((ROWS,...  1.95 us
  transfers between devices with their start and end apart: 7, of which 6 were waited for; matrix products, arithmetic and copies ran while one was open for 0% of the time, Pallas kernels for 12%

profile of v4, /device:TPU:0, one launch (start us, length us, event | category | flops | bytes accessed | tf_op | source)
XLA Modules:
  0.0 66.9 jit_solution(15051577705393386179)
XLA Ops:
  0.6 0.0 copy-start
  0.6 0.0 copy-start.1
  0.7 1.0 %copy-done.1 = bf16[32,5184]{1,0:T(8,128)(2,1)S(1)} copy-done((bf16[32,5184]{1,0:T(8,128)(2,1)S(1)}, bf16[32,5184]{1,0:T(8,128)(2,1)}, u32[]{:S(2)}) %copy-start.1) | copy-done | bytes 331800
  1.7 0.0 copy-start.2
  1.7 0.0 copy-start.3
  1.7 1.5 %shard_map.76 = (bf16[288,576]{1,0:T(8,128)(2,1)S(1)}, bf16[2,288,288]{2,1,0:T(8,128)(2,1)S(1)}) custom-call(bf16[32,5184]{1,0:T(8,128)(2,1)S(1)} %copy-done.1), custom_call_target="tpu_custom_call" | custom-call | flops 1358954496 | bytes 3145728 | tf_op jit(solution)/shard_map/pallas_call | solution.py:228
  3.2 0.0 copy-done.2
  3.2 0.0 copy-done.3
  3.2 2.0 %shard_map.77 = (f32[8,2,32,512]{3,2,1,0:T(8,128)S(1)}, bf16[8,32,512]{2,1,0:T(8,128)(2,1)S(1)}, bf16[2,512]{1,0:T(2,128)(2,1)S(1)}) custom-call(bf16[32,8,512]{2,1,0:T(8,128)(2,1)S(1)} %copy-done.2, bf16[2,288,288]{2,1,0:T(8,128)(2,1)S(1)} %get-tuple-element.19.a_ref, s32[8,512]{1,0:T(8,128)S(1)} %copy-done.3), custom_call_target="tpu_custom_call" | custom-call | flops 679477248 | bytes 3145728 | tf_op jit(solution)/shard_map/pallas_call | solution.py:250
  5.1 0.1 convert_element_type.47
  5.3 0.1 collective-permute-start
  5.4 0.0 copy-done
  5.4 0.1 constant_dynamic-slice_fusion
  5.5 1.8 %shard_map.78 = f32[8,2,32,512]{3,2,1,0:T(8,128)S(1)} custom-call(bf16[8,32,512]{2,1,0:T(8,128)(2,1)S(1)} %get-tuple-element.20.rows_ref.coef_ref, bf16[2,288,288]{2,1,0:T(8,128)(2,1)S(1)} %get-tuple-element.19.a_ref, bf16[2,512]{1,0:T(2,128)(2,1)S(1)} %get-tuple-element.21.edge_ref), custom_call_target="tpu_custom_call" | custom-call | flops 679477248 | bytes 3145728 | tf_op jit(solution)/shard_map/pallas_call | solution.py:263
  7.3 0.0 collective-permute-done
  7.3 0.2 add_convert_fusion
  7.5 16.7 %all_to_all.10 = f16[8,2,32,512]{3,2,1,0:T(8,128)(2,1)S(1)} all-to-all(f16[8,2,32,512]{3,2,1,0:T(8,128)(2,1)S(1)} %add_convert_fusion), channel_id=1, replica_groups={{0,2,4,6,8,10,12,14},{1,3,5,7,9,11,13,15},{16,18,20,22,24,26,28,30},{17..., dimensions={0} | all-to-all | bytes 1048576 | tf_op jit(solution)/shard_map/all_to_all | solution.py:223
  24.2 0.1 convert_reduce_fusion
  24.3 0.0 copy-start.4
  24.3 4.6 %collective-permute-start.1 = (f32[2,32,512]{2,1,0:T(8,128)S(1)}, f32[2,32,512]{2,1,0:T(8,128)S(1)}, u32[]{:S(2)}, u32[]{:S(2)}) collective-permute-start(f32[2,32,512]{2,1,0:T(8,128)S(1)} %pad_maximum_fusion.1), channel_id=1, source_target_pairs={{0,120},{1,121},{2,122},{3,123},{4,124},{5,125},{6,126},{7,127},{8... | collective-permute-start | bytes 393224 | tf_op jit(solution)/shard_map/ppermute | solution.py:280
  28.9 3.8 %collective-permute-done.1 = f32[2,32,512]{2,1,0:T(8,128)S(1)} collective-permute-done((f32[2,32,512]{2,1,0:T(8,128)S(1)}, f32[2,32,512]{2,1,0:T(8,128)S(1)}, u32[]{:S(2)}, u32[]{:S(2)}) %collective-permute-start.1) | collective-permute-done | bytes 131104 | tf_op jit(solution)/shard_map/ppermute | solution.py:280
  32.7 0.0 copy-done.4
  32.7 0.1 broadcast_in_dim.8.shrink_ref
  32.9 11.7 %all_to_all.11.half_ref.mine_ref = bf16[8,2,32,512]{3,2,1,0:T(8,128)(2,1)S(1)} all-to-all(bf16[8,2,32,512]{3,2,1,0:T(8,128)(2,1)S(1)} %broadcast_in_dim.9), channel_id=1, replica_groups={{0,2,4,6,8,10,12,14},{1,3,5,7,9,11,13,15},{16,18,20,22,24,26,28,30},{17..., dimensions={0} | all-to-all | bytes 1048576 | tf_op jit(solution)/shard_map/all_to_all | solution.py:223
  44.6 0.0 collective-permute-start.2
  44.6 1.7 %shard_map.79 = f32[4,88,256]{2,1,0:T(8,128)S(1)} custom-call(bf16[8,2,32,512]{3,2,1,0:T(8,128)(2,1)S(1)} %all_to_all.11.half_ref.mine_ref, bf16[2,512]{1,0:T(2,128)(2,1)S(1)} %get-tuple-element.21.edge_ref, bf16[8,32,512]{2,1,0:T(8,128)(2,1)S(1)} %get-tuple-element.20.rows_ref.coef_ref), custom_call_target="tpu_custom_call" | custom-call | flops 679477248 | bytes 3145728 | tf_op jit(solution)/shard_map/pallas_call | solution.py:301
  46.3 0.2 collective-permute-done.2.half_ref.other_ref
  46.5 1.7 %shard_map.80 = f32[4,88,256]{2,1,0:T(8,128)S(1)} custom-call(bf16[8,2,32,512]{3,2,1,0:T(8,128)(2,1)S(1)} %collective-permute-done.2.half_ref.other_ref, bf16[2,512]{1,0:T(2,128)(2,1)S(1)} %get-tuple-element.21.edge_ref, bf16[8,32,512]{2,1,0:T(8,128)(2,1)S(1)} %get-tuple-element.20.rows_ref.coef_ref), custom_call_target="tpu_custom_call" | custom-call | flops 679477248 | bytes 3145728 | tf_op jit(solution)/shard_map/pallas_call | solution.py:302
  48.2 0.1 broadcast_select_fusion.1
  48.4 2.6 %collective-permute-start.3 = (f16[4,88,256]{2,1,0:T(8,128)(2,1)S(1)}, f16[4,88,256]{2,1,0:T(8,128)(2,1)S(1)}, u32[]{:S(2)}, u32[]{:S(2)}) collective-permute-start(f16[4,88,256]{2,1,0:T(8,128)(2,1)S(1)} %fusion.1), channel_id=1, source_target_pairs={{0,16},{16,0},{32,48},{48,32},{64,80},{80,64},{96,112},{112,96},{1... | collective-permute-start | bytes 540680 | tf_op jit(solution)/shard_map/ppermute | solution.py:310
  51.1 4.3 %shard_map.81 = (bf16[32,8,512]{2,1,0:T(8,128)(2,1)}, bf16[64,8,512]{2,1,0:T(8,128)(2,1)}) custom-call(bf16[8,2,32,512]{3,2,1,0:T(8,128)(2,1)S(1)} %all_to_all.11.half_ref.mine_ref, bf16[8,2,32,512]{3,2,1,0:T(8,128)(2,1)S(1)} %collective-permute-done.2.half_ref.other_ref, bf16[2,512]{1,0:T(2,128)(2,1)S(1)} %get-tuple-element.21.edge_ref, ...), custom_call_target="tpu_custom_call" | custom-call | flops 1358954496 | bytes 3145728 | tf_op jit(solution)/shard_map/pallas_call | solution.py:311
  55.4 1.6 %collective-permute-done.3 = f16[4,88,256]{2,1,0:T(8,128)(2,1)S(1)} collective-permute-done((f16[4,88,256]{2,1,0:T(8,128)(2,1)S(1)}, f16[4,88,256]{2,1,0:T(8,128)(2,1)S(1)}, u32[]{:S(2)}, u32[]{:S(2)}) %collective-permute-start.3) | collective-permute-done | bytes 180256 | tf_op jit(solution)/shard_map/ppermute | solution.py:310
  57.0 0.1 fusion
  57.0 0.1 fusion.2
  57.2 2.4 %collective-permute-start.4 = (f16[88,256]{1,0:T(8,128)(2,1)S(1)}, f16[88,256]{1,0:T(8,128)(2,1)S(1)}, u32[]{:S(2)}, u32[]{:S(2)}) collective-permute-start(f16[88,256]{1,0:T(8,128)(2,1)S(1)} %get-tuple-element.42), channel_id=1, source_target_pairs={{0,64},{16,80},{32,96},{48,112},{64,0},{80,16},{96,32},{112,48},{1... | collective-permute-start | bytes 135176 | tf_op jit(solution)/shard_map/ppermute | solution.py:337
  59.6 1.9 %collective-permute-start.5 = (f16[88,256]{1,0:T(8,128)(2,1)S(1)}, f16[88,256]{1,0:T(8,128)(2,1)S(1)}, u32[]{:S(2)}, u32[]{:S(2)}) collective-permute-start(f16[88,256]{1,0:T(8,128)(2,1)S(1)} %get-tuple-element.43), channel_id=1, source_target_pairs={{0,32},{16,48},{32,64},{48,80},{64,96},{80,112},{96,0},{112,16},{1... | collective-permute-start | bytes 135176 | tf_op jit(solution)/shard_map/ppermute | solution.py:337
  61.5 1.4 %collective-permute-start.6 = (f16[88,256]{1,0:T(8,128)(2,1)S(1)}, f16[88,256]{1,0:T(8,128)(2,1)S(1)}, u32[]{:S(2)}, u32[]{:S(2)}) collective-permute-start(f16[88,256]{1,0:T(8,128)(2,1)S(1)} %get-tuple-element.44), channel_id=1, source_target_pairs={{0,96},{16,112},{32,0},{48,16},{64,32},{80,48},{96,64},{112,80},{1... | collective-permute-start | bytes 135176 | tf_op jit(solution)/shard_map/ppermute | solution.py:337
  62.8 0.2 collective-permute-done.4
  63.0 1.8 %collective-permute-done.5 = f16[88,256]{1,0:T(8,128)(2,1)S(1)} collective-permute-done((f16[88,256]{1,0:T(8,128)(2,1)S(1)}, f16[88,256]{1,0:T(8,128)(2,1)S(1)}, u32[]{:S(2)}, u32[]{:S(2)}) %collective-permute-start.5) | collective-permute-done | bytes 45088 | tf_op jit(solution)/shard_map/ppermute | solution.py:337
  64.9 0.7 %collective-permute-done.6 = f16[88,256]{1,0:T(8,128)(2,1)S(1)} collective-permute-done((f16[88,256]{1,0:T(8,128)(2,1)S(1)}, f16[88,256]{1,0:T(8,128)(2,1)S(1)}, u32[]{:S(2)}, u32[]{:S(2)}) %collective-permute-start.6) | collective-permute-done | bytes 45088 | tf_op jit(solution)/shard_map/ppermute | solution.py:337
  65.6 0.1 reshape.43
  65.7 0.1 reshape.42
  65.8 0.2 copy.18
  66.1 0.8 %copy.19 = f32[32,648]{1,0:T(8,128)} copy(f32[32,648]{0,1:T(8,128)S(1)} %reshape.44) | data formatting | bytes 165888
  (17 shorter events, 0.4 us)
Async XLA Ops:
  0.6 4.8 %copy-start = (bf16[64,8,512]{2,1,0:T(8,128)(2,1)S(1)}, bf16[64,8,512]{2,1,0:T(8,128)(2,1)}, u32[]{:S(2)}) copy-start(bf16[64,8,512]{2,1,0:T(8,128)(2,1)} %param.5) | copy-start | bytes 1572868
  0.6 1.0 %copy-start.1 = (bf16[32,5184]{1,0:T(8,128)(2,1)S(1)}, bf16[32,5184]{1,0:T(8,128)(2,1)}, u32[]{:S(2)}) copy-start(bf16[32,5184]{1,0:T(8,128)(2,1)} %d_ref.1) | copy-start | bytes 995332
  1.7 1.5 %copy-start.2 = (bf16[32,8,512]{2,1,0:T(8,128)(2,1)S(1)}, bf16[32,8,512]{2,1,0:T(8,128)(2,1)}, u32[]{:S(2)}) copy-start(bf16[32,8,512]{2,1,0:T(8,128)(2,1)} %coef_ref.1) | copy-start | bytes 786436
  1.7 1.5 %copy-start.3 = (s32[8,512]{1,0:T(8,128)S(1)}, s32[8,512]{1,0:T(8,128)}, u32[]{:S(2)}) copy-start(s32[8,512]{1,0:T(8,128)} %seam_ref.1) | copy-start | bytes 49156
  5.3 2.1 %collective-permute-start = (f16[8,2,32,512]{3,2,1,0:T(8,128)(2,1)S(1)}, f16[8,2,32,512]{3,2,1,0:T(8,128)(2,1)S(1)}, u32[]{:S(2)}, u32[]{:S(2)}) collective-permute-start(f16[8,2,32,512]{3,2,1,0:T(8,128)(2,1)S(1)} %convert_element_type.47), channel_id=1, source_target_pairs={{0,1},{1,0},{2,3},{3,2},{4,5},{5,4},{6,7},{7,6},{8,9},{9,8},{10,11... | collective-permute-start | bytes 1572872 | tf_op jit(solution)/shard_map/ppermute | solution.py:273
  24.3 8.4 %copy-start.4 = (f32[32]{0:T(128)S(1)}, f32[32]{0:T(128)}, u32[]{:S(2)}) copy-start(f32[32]{0:T(128)} %param.8) | copy-start | bytes 388
  24.3 8.4 %collective-permute-start.1 = (f32[2,32,512]{2,1,0:T(8,128)S(1)}, f32[2,32,512]{2,1,0:T(8,128)S(1)}, u32[]{:S(2)}, u32[]{:S(2)}) collective-permute-start(f32[2,32,512]{2,1,0:T(8,128)S(1)} %pad_maximum_fusion.1), channel_id=1, source_target_pairs={{0,120},{1,121},{2,122},{3,123},{4,124},{5,125},{6,126},{7,127},{8... | collective-permute-start | bytes 393224 | tf_op jit(solution)/shard_map/ppermute | solution.py:280
  44.6 1.9 %collective-permute-start.2 = (bf16[8,2,32,512]{3,2,1,0:T(8,128)(2,1)S(1)}, bf16[8,2,32,512]{3,2,1,0:T(8,128)(2,1)S(1)}, u32[]{:S(2)}, u32[]{:S(2)}) collective-permute-start(bf16[8,2,32,512]{3,2,1,0:T(8,128)(2,1)S(1)} %all_to_all.11.half_ref.mine_ref), channel_id=1, source_target_pairs={{0,1},{1,0},{2,3},{3,2},{4,5},{5,4},{6,7},{7,6},{8,9},{9,8},{10,11... | collective-permute-start | bytes 1572872 | tf_op jit(solution)/shard_map/ppermute | solution.py:285
  48.4 8.6 %collective-permute-start.3 = (f16[4,88,256]{2,1,0:T(8,128)(2,1)S(1)}, f16[4,88,256]{2,1,0:T(8,128)(2,1)S(1)}, u32[]{:S(2)}, u32[]{:S(2)}) collective-permute-start(f16[4,88,256]{2,1,0:T(8,128)(2,1)S(1)} %fusion.1), channel_id=1, source_target_pairs={{0,16},{16,0},{32,48},{48,32},{64,80},{80,64},{96,112},{112,96},{1... | collective-permute-start | bytes 540680 | tf_op jit(solution)/shard_map/ppermute | solution.py:310
  57.2 5.9 %collective-permute-start.4 = (f16[88,256]{1,0:T(8,128)(2,1)S(1)}, f16[88,256]{1,0:T(8,128)(2,1)S(1)}, u32[]{:S(2)}, u32[]{:S(2)}) collective-permute-start(f16[88,256]{1,0:T(8,128)(2,1)S(1)} %get-tuple-element.42), channel_id=1, source_target_pairs={{0,64},{16,80},{32,96},{48,112},{64,0},{80,16},{96,32},{112,48},{1... | collective-permute-start | bytes 135176 | tf_op jit(solution)/shard_map/ppermute | solution.py:337
  59.6 5.3 %collective-permute-start.5 = (f16[88,256]{1,0:T(8,128)(2,1)S(1)}, f16[88,256]{1,0:T(8,128)(2,1)S(1)}, u32[]{:S(2)}, u32[]{:S(2)}) collective-permute-start(f16[88,256]{1,0:T(8,128)(2,1)S(1)} %get-tuple-element.43), channel_id=1, source_target_pairs={{0,32},{16,48},{32,64},{48,80},{64,96},{80,112},{96,0},{112,16},{1... | collective-permute-start | bytes 135176 | tf_op jit(solution)/shard_map/ppermute | solution.py:337
  61.5 4.0 %collective-permute-start.6 = (f16[88,256]{1,0:T(8,128)(2,1)S(1)}, f16[88,256]{1,0:T(8,128)(2,1)S(1)}, u32[]{:S(2)}, u32[]{:S(2)}) collective-permute-start(f16[88,256]{1,0:T(8,128)(2,1)S(1)} %get-tuple-element.44), channel_id=1, source_target_pairs={{0,96},{16,112},{32,0},{48,16},{64,32},{80,48},{96,64},{112,80},{1... | collective-permute-start | bytes 135176 | tf_op jit(solution)/shard_map/ppermute | solution.py:337

commit v5 on v4

--- a/solution.py
+++ b/solution.py
@@ -276,10 +276,11 @@
     pieces = exchange(partial)
     total = jnp.sum(pieces.astype(jnp.float32), axis=0)
     held = jnp.stack([image_row.astype(jnp.float32) - total[0], total[1]])
-    held, shrink = lax.optimization_barrier((held, shrink))
+    held, shrink = lax.optimization_barrier((held.astype(jnp.float16), shrink))
     facing = lax.ppermute(held, ("tile", "atom"), pairs)
     threshold = jnp.broadcast_to(shrink[:, None], (atoms, 128))
     facing, threshold = lax.optimization_barrier((facing, threshold))
+    held, facing = held.astype(jnp.float32), facing.astype(jnp.float32)
     rows_two = jnp.stack([held[0] - facing[1], facing[0] - held[1]]).astype(jnp.bfloat16)
     mine = exchange(jnp.broadcast_to(rows_two[None], (ROWS, 2, HALF, TILE_W)))
     theirs = lax.ppermute(mine, "atom", swap)

time: 67.2 us -> 65.8 us (0.979)
  blocking collectives: 28.4 us -> 27.7 us
    ppermute x1, waiting for transfers between devices: 3.81 us -> 3.09 us  [per_device(): facing = lax.ppermute(held, ('tile', 'atom'), pairs)]
    all_to_all x2, blocking collectives: 28.4 us -> 27.7 us  [exchange(): lax.all_to_all(field, 'atom', 0, 0, tiled=True, axis_index_groups=chips)]
where the time goes in v5:
time: 65.8 us; the launch traced here: 65.4 us
  blocking collectives  27.7 us (42%)
  Pallas kernels  13 us (20%)
  starting transfers between devices  12.7 us (19%)
  waiting for transfers between devices  7.66 us (12%)
  local copies, waits for them, and re-layouts  2.48 us (4%)
  between operations  0.96 us (1%)
  other arithmetic  0.88 us (1%)
    all_to_all x2, blocking collectives, exchange(): lax.all_to_all(field, 'atom', 0, 0, tiled=True, axis_index_groups=chips)  27.7 us
    ppermute x3, starting transfers between devices, per_device(): got.append(lax.ppermute(ahead[hops], 'tile', route))  5.56 us
    ppermute x1, starting transfers between devices, per_device(): facing = lax.ppermute(held, ('tile', 'atom'), pairs)  4.56 us
    pallas_call x1, Pallas kernels, per_device(): pl.pallas_call(coeffs_kernel, out_shape=(jax.ShapeDtypeStruct((atoms, ROW...  4.32 us
    ppermute x1, waiting for transfers between devices, per_device(): facing = lax.ppermute(held, ('tile', 'atom'), pairs)  3.09 us
    ppermute x3, waiting for transfers between devices, per_device(): got.append(lax.ppermute(ahead[hops], 'tile', route))  2.7 us
    ppermute x1, starting transfers between devices, per_device(): across = lax.ppermute(away, 'tile', [(i, i ^ 1) for i in range(strips)])  2.55 us
    pallas_call x1, Pallas kernels, per_device(): pl.pallas_call(send_kernel, out_shape=(sums, jax.ShapeDtypeStruct((ROWS,...  1.95 us
  transfers between devices with their start and end apart: 7, of which 6 were waited for; matrix products, arithmetic and copies ran while one was open for 0% of the time, Pallas kernels for 12%

profile of v5, /device:TPU:0, one launch (start us, length us, event | category | flops | bytes accessed | tf_op | source)
XLA Modules:
  0.0 65.4 jit_solution(16502089923745949495)
XLA Ops:
  0.6 0.0 copy-start
  0.6 0.0 copy-start.1
  0.7 1.0 %copy-done.1 = bf16[32,5184]{1,0:T(8,128)(2,1)S(1)} copy-done((bf16[32,5184]{1,0:T(8,128)(2,1)S(1)}, bf16[32,5184]{1,0:T(8,128)(2,1)}, u32[]{:S(2)}) %copy-start.1) | copy-done | bytes 331800
  1.7 0.0 copy-start.2
  1.7 0.0 copy-start.3
  1.7 1.5 %shard_map.76 = (bf16[288,576]{1,0:T(8,128)(2,1)S(1)}, bf16[2,288,288]{2,1,0:T(8,128)(2,1)S(1)}) custom-call(bf16[32,5184]{1,0:T(8,128)(2,1)S(1)} %copy-done.1), custom_call_target="tpu_custom_call" | custom-call | flops 1358954496 | bytes 3145728 | tf_op jit(solution)/shard_map/pallas_call | solution.py:228
  3.2 0.0 copy-done.2
  3.2 0.0 copy-done.3
  3.2 2.0 %shard_map.77 = (f32[8,2,32,512]{3,2,1,0:T(8,128)S(1)}, bf16[8,32,512]{2,1,0:T(8,128)(2,1)S(1)}, bf16[2,512]{1,0:T(2,128)(2,1)S(1)}) custom-call(bf16[32,8,512]{2,1,0:T(8,128)(2,1)S(1)} %copy-done.2, bf16[2,288,288]{2,1,0:T(8,128)(2,1)S(1)} %get-tuple-element.19.a_ref, s32[8,512]{1,0:T(8,128)S(1)} %copy-done.3), custom_call_target="tpu_custom_call" | custom-call | flops 679477248 | bytes 3145728 | tf_op jit(solution)/shard_map/pallas_call | solution.py:250
  5.1 0.1 convert_element_type.54
  5.3 0.1 collective-permute-start
  5.4 0.0 copy-done
  5.4 0.1 constant_dynamic-slice_fusion
  5.5 1.8 %shard_map.78 = f32[8,2,32,512]{3,2,1,0:T(8,128)S(1)} custom-call(bf16[8,32,512]{2,1,0:T(8,128)(2,1)S(1)} %get-tuple-element.20.rows_ref.coef_ref, bf16[2,288,288]{2,1,0:T(8,128)(2,1)S(1)} %get-tuple-element.19.a_ref, bf16[2,512]{1,0:T(2,128)(2,1)S(1)} %get-tuple-element.21.edge_ref), custom_call_target="tpu_custom_call" | custom-call | flops 679477248 | bytes 3145728 | tf_op jit(solution)/shard_map/pallas_call | solution.py:263
  7.3 0.0 collective-permute-done
  7.3 0.2 add_convert_fusion
  7.5 16.7 %all_to_all.10 = f16[8,2,32,512]{3,2,1,0:T(8,128)(2,1)S(1)} all-to-all(f16[8,2,32,512]{3,2,1,0:T(8,128)(2,1)S(1)} %add_convert_fusion), channel_id=1, replica_groups={{0,2,4,6,8,10,12,14},{1,3,5,7,9,11,13,15},{16,18,20,22,24,26,28,30},{17..., dimensions={0} | all-to-all | bytes 1048576 | tf_op jit(solution)/shard_map/all_to_all | solution.py:223
  24.2 0.1 convert_reduce_fusion
  24.3 0.0 copy-start.4
  24.4 4.6 %collective-permute-start.1 = (f16[2,32,512]{2,1,0:T(8,128)(2,1)S(1)}, f16[2,32,512]{2,1,0:T(8,128)(2,1)S(1)}, u32[]{:S(2)}, u32[]{:S(2)}) collective-permute-start(f16[2,32,512]{2,1,0:T(8,128)(2,1)S(1)} %pad_maximum_fusion.1), channel_id=1, source_target_pairs={{0,120},{1,121},{2,122},{3,123},{4,124},{5,125},{6,126},{7,127},{8... | collective-permute-start | bytes 196616 | tf_op jit(solution)/shard_map/ppermute | solution.py:280
  28.9 3.1 %collective-permute-done.1 = f16[2,32,512]{2,1,0:T(8,128)(2,1)S(1)} collective-permute-done((f16[2,32,512]{2,1,0:T(8,128)(2,1)S(1)}, f16[2,32,512]{2,1,0:T(8,128)(2,1)S(1)}, u32[]{:S(2)}, u32[]{:S(2)}) %collective-permute-start.1) | collective-permute-done | bytes 65568 | tf_op jit(solution)/shard_map/ppermute | solution.py:280
  32.0 0.0 copy-done.4
  32.0 0.1 broadcast_in_dim.8.shrink_ref
  32.2 11.0 %all_to_all.11.half_ref.mine_ref = bf16[8,2,32,512]{3,2,1,0:T(8,128)(2,1)S(1)} all-to-all(bf16[8,2,32,512]{3,2,1,0:T(8,128)(2,1)S(1)} %broadcast_in_dim.9), channel_id=1, replica_groups={{0,2,4,6,8,10,12,14},{1,3,5,7,9,11,13,15},{16,18,20,22,24,26,28,30},{17..., dimensions={0} | all-to-all | bytes 1048576 | tf_op jit(solution)/shard_map/all_to_all | solution.py:223
  43.3 0.0 collective-permute-start.2
  43.3 1.7 %shard_map.79 = f32[4,88,256]{2,1,0:T(8,128)S(1)} custom-call(bf16[8,2,32,512]{3,2,1,0:T(8,128)(2,1)S(1)} %all_to_all.11.half_ref.mine_ref, bf16[2,512]{1,0:T(2,128)(2,1)S(1)} %get-tuple-element.21.edge_ref, bf16[8,32,512]{2,1,0:T(8,128)(2,1)S(1)} %get-tuple-element.20.rows_ref.coef_ref), custom_call_target="tpu_custom_call" | custom-call | flops 679477248 | bytes 3145728 | tf_op jit(solution)/shard_map/pallas_call | solution.py:302
  45.0 0.2 collective-permute-done.2.half_ref.other_ref
  45.2 1.7 %shard_map.80 = f32[4,88,256]{2,1,0:T(8,128)S(1)} custom-call(bf16[8,2,32,512]{3,2,1,0:T(8,128)(2,1)S(1)} %collective-permute-done.2.half_ref.other_ref, bf16[2,512]{1,0:T(2,128)(2,1)S(1)} %get-tuple-element.21.edge_ref, bf16[8,32,512]{2,1,0:T(8,128)(2,1)S(1)} %get-tuple-element.20.rows_ref.coef_ref), custom_call_target="tpu_custom_call" | custom-call | flops 679477248 | bytes 3145728 | tf_op jit(solution)/shard_map/pallas_call | solution.py:303
  46.9 0.1 broadcast_select_fusion.1
  47.1 2.5 %collective-permute-start.3 = (f16[4,88,256]{2,1,0:T(8,128)(2,1)S(1)}, f16[4,88,256]{2,1,0:T(8,128)(2,1)S(1)}, u32[]{:S(2)}, u32[]{:S(2)}) collective-permute-start(f16[4,88,256]{2,1,0:T(8,128)(2,1)S(1)} %fusion.1), channel_id=1, source_target_pairs={{0,16},{16,0},{32,48},{48,32},{64,80},{80,64},{96,112},{112,96},{1... | collective-permute-start | bytes 540680 | tf_op jit(solution)/shard_map/ppermute | solution.py:311
  49.6 4.3 %shard_map.81 = (bf16[32,8,512]{2,1,0:T(8,128)(2,1)}, bf16[64,8,512]{2,1,0:T(8,128)(2,1)}) custom-call(bf16[8,2,32,512]{3,2,1,0:T(8,128)(2,1)S(1)} %all_to_all.11.half_ref.mine_ref, bf16[8,2,32,512]{3,2,1,0:T(8,128)(2,1)S(1)} %collective-permute-done.2.half_ref.other_ref, bf16[2,512]{1,0:T(2,128)(2,1)S(1)} %get-tuple-element.21.edge_ref, ...), custom_call_target="tpu_custom_call" | custom-call | flops 1358954496 | bytes 3145728 | tf_op jit(solution)/shard_map/pallas_call | solution.py:312
  53.9 1.7 %collective-permute-done.3 = f16[4,88,256]{2,1,0:T(8,128)(2,1)S(1)} collective-permute-done((f16[4,88,256]{2,1,0:T(8,128)(2,1)S(1)}, f16[4,88,256]{2,1,0:T(8,128)(2,1)S(1)}, u32[]{:S(2)}, u32[]{:S(2)}) %collective-permute-start.3) | collective-permute-done | bytes 180256 | tf_op jit(solution)/shard_map/ppermute | solution.py:311
  55.6 0.1 fusion
  55.7 0.1 fusion.2
  55.8 2.3 %collective-permute-start.4 = (f16[88,256]{1,0:T(8,128)(2,1)S(1)}, f16[88,256]{1,0:T(8,128)(2,1)S(1)}, u32[]{:S(2)}, u32[]{:S(2)}) collective-permute-start(f16[88,256]{1,0:T(8,128)(2,1)S(1)} %get-tuple-element.42), channel_id=1, source_target_pairs={{0,64},{16,80},{32,96},{48,112},{64,0},{80,16},{96,32},{112,48},{1... | collective-permute-start | bytes 135176 | tf_op jit(solution)/shard_map/ppermute | solution.py:338
  58.1 1.9 %collective-permute-start.5 = (f16[88,256]{1,0:T(8,128)(2,1)S(1)}, f16[88,256]{1,0:T(8,128)(2,1)S(1)}, u32[]{:S(2)}, u32[]{:S(2)}) collective-permute-start(f16[88,256]{1,0:T(8,128)(2,1)S(1)} %get-tuple-element.43), channel_id=1, source_target_pairs={{0,32},{16,48},{32,64},{48,80},{64,96},{80,112},{96,0},{112,16},{1... | collective-permute-start | bytes 135176 | tf_op jit(solution)/shard_map/ppermute | solution.py:338
  60.0 1.3 %collective-permute-start.6 = (f16[88,256]{1,0:T(8,128)(2,1)S(1)}, f16[88,256]{1,0:T(8,128)(2,1)S(1)}, u32[]{:S(2)}, u32[]{:S(2)}) collective-permute-start(f16[88,256]{1,0:T(8,128)(2,1)S(1)} %get-tuple-element.44), channel_id=1, source_target_pairs={{0,96},{16,112},{32,0},{48,16},{64,32},{80,48},{96,64},{112,80},{1... | collective-permute-start | bytes 135176 | tf_op jit(solution)/shard_map/ppermute | solution.py:338
  61.4 0.4 collective-permute-done.4
  61.8 1.6 %collective-permute-done.5 = f16[88,256]{1,0:T(8,128)(2,1)S(1)} collective-permute-done((f16[88,256]{1,0:T(8,128)(2,1)S(1)}, f16[88,256]{1,0:T(8,128)(2,1)S(1)}, u32[]{:S(2)}, u32[]{:S(2)}) %collective-permute-start.5) | collective-permute-done | bytes 45088 | tf_op jit(solution)/shard_map/ppermute | solution.py:338
  63.4 0.7 %collective-permute-done.6 = f16[88,256]{1,0:T(8,128)(2,1)S(1)} collective-permute-done((f16[88,256]{1,0:T(8,128)(2,1)S(1)}, f16[88,256]{1,0:T(8,128)(2,1)S(1)}, u32[]{:S(2)}, u32[]{:S(2)}) %collective-permute-start.6) | collective-permute-done | bytes 45088 | tf_op jit(solution)/shard_map/ppermute | solution.py:338
  64.1 0.1 reshape.43
  64.2 0.1 reshape.42
  64.3 0.2 copy.18
  64.7 0.8 %copy.19 = f32[32,648]{1,0:T(8,128)} copy(f32[32,648]{0,1:T(8,128)S(1)} %reshape.44) | data formatting | bytes 165888
  (19 shorter events, 0.4 us)
Async XLA Ops:
  0.6 4.8 %copy-start = (bf16[64,8,512]{2,1,0:T(8,128)(2,1)S(1)}, bf16[64,8,512]{2,1,0:T(8,128)(2,1)}, u32[]{:S(2)}) copy-start(bf16[64,8,512]{2,1,0:T(8,128)(2,1)} %param.5) | copy-start | bytes 1572868
  0.6 1.0 %copy-start.1 = (bf16[32,5184]{1,0:T(8,128)(2,1)S(1)}, bf16[32,5184]{1,0:T(8,128)(2,1)}, u32[]{:S(2)}) copy-start(bf16[32,5184]{1,0:T(8,128)(2,1)} %d_ref.1) | copy-start | bytes 995332
  1.7 1.5 %copy-start.2 = (bf16[32,8,512]{2,1,0:T(8,128)(2,1)S(1)}, bf16[32,8,512]{2,1,0:T(8,128)(2,1)}, u32[]{:S(2)}) copy-start(bf16[32,8,512]{2,1,0:T(8,128)(2,1)} %coef_ref.1) | copy-start | bytes 786436
  1.7 1.5 %copy-start.3 = (s32[8,512]{1,0:T(8,128)S(1)}, s32[8,512]{1,0:T(8,128)}, u32[]{:S(2)}) copy-start(s32[8,512]{1,0:T(8,128)} %seam_ref.1) | copy-start | bytes 49156
  5.3 2.1 %collective-permute-start = (f16[8,2,32,512]{3,2,1,0:T(8,128)(2,1)S(1)}, f16[8,2,32,512]{3,2,1,0:T(8,128)(2,1)S(1)}, u32[]{:S(2)}, u32[]{:S(2)}) collective-permute-start(f16[8,2,32,512]{3,2,1,0:T(8,128)(2,1)S(1)} %convert_element_type.54), channel_id=1, source_target_pairs={{0,1},{1,0},{2,3},{3,2},{4,5},{5,4},{6,7},{7,6},{8,9},{9,8},{10,11... | collective-permute-start | bytes 1572872 | tf_op jit(solution)/shard_map/ppermute | solution.py:273
  24.3 7.7 %copy-start.4 = (f32[32]{0:T(128)S(1)}, f32[32]{0:T(128)}, u32[]{:S(2)}) copy-start(f32[32]{0:T(128)} %param.8) | copy-start | bytes 388
  24.4 7.7 %collective-permute-start.1 = (f16[2,32,512]{2,1,0:T(8,128)(2,1)S(1)}, f16[2,32,512]{2,1,0:T(8,128)(2,1)S(1)}, u32[]{:S(2)}, u32[]{:S(2)}) collective-permute-start(f16[2,32,512]{2,1,0:T(8,128)(2,1)S(1)} %pad_maximum_fusion.1), channel_id=1, source_target_pairs={{0,120},{1,121},{2,122},{3,123},{4,124},{5,125},{6,126},{7,127},{8... | collective-permute-start | bytes 196616 | tf_op jit(solution)/shard_map/ppermute | solution.py:280
  43.3 1.9 %collective-permute-start.2 = (bf16[8,2,32,512]{3,2,1,0:T(8,128)(2,1)S(1)}, bf16[8,2,32,512]{3,2,1,0:T(8,128)(2,1)S(1)}, u32[]{:S(2)}, u32[]{:S(2)}) collective-permute-start(bf16[8,2,32,512]{3,2,1,0:T(8,128)(2,1)S(1)} %all_to_all.11.half_ref.mine_ref), channel_id=1, source_target_pairs={{0,1},{1,0},{2,3},{3,2},{4,5},{5,4},{6,7},{7,6},{8,9},{9,8},{10,11... | collective-permute-start | bytes 1572872 | tf_op jit(solution)/shard_map/ppermute | solution.py:286
  47.1 8.5 %collective-permute-start.3 = (f16[4,88,256]{2,1,0:T(8,128)(2,1)S(1)}, f16[4,88,256]{2,1,0:T(8,128)(2,1)S(1)}, u32[]{:S(2)}, u32[]{:S(2)}) collective-permute-start(f16[4,88,256]{2,1,0:T(8,128)(2,1)S(1)} %fusion.1), channel_id=1, source_target_pairs={{0,16},{16,0},{32,48},{48,32},{64,80},{80,64},{96,112},{112,96},{1... | collective-permute-start | bytes 540680 | tf_op jit(solution)/shard_map/ppermute | solution.py:311
  55.8 6.0 %collective-permute-start.4 = (f16[88,256]{1,0:T(8,128)(2,1)S(1)}, f16[88,256]{1,0:T(8,128)(2,1)S(1)}, u32[]{:S(2)}, u32[]{:S(2)}) collective-permute-start(f16[88,256]{1,0:T(8,128)(2,1)S(1)} %get-tuple-element.42), channel_id=1, source_target_pairs={{0,64},{16,80},{32,96},{48,112},{64,0},{80,16},{96,32},{112,48},{1... | collective-permute-start | bytes 135176 | tf_op jit(solution)/shard_map/ppermute | solution.py:338
  58.1 5.3 %collective-permute-start.5 = (f16[88,256]{1,0:T(8,128)(2,1)S(1)}, f16[88,256]{1,0:T(8,128)(2,1)S(1)}, u32[]{:S(2)}, u32[]{:S(2)}) collective-permute-start(f16[88,256]{1,0:T(8,128)(2,1)S(1)} %get-tuple-element.43), channel_id=1, source_target_pairs={{0,32},{16,48},{32,64},{48,80},{64,96},{80,112},{96,0},{112,16},{1... | collective-permute-start | bytes 135176 | tf_op jit(solution)/shard_map/ppermute | solution.py:338
  60.0 4.0 %collective-permute-start.6 = (f16[88,256]{1,0:T(8,128)(2,1)S(1)}, f16[88,256]{1,0:T(8,128)(2,1)S(1)}, u32[]{:S(2)}, u32[]{:S(2)}) collective-permute-start(f16[88,256]{1,0:T(8,128)(2,1)S(1)} %get-tuple-element.44), channel_id=1, source_target_pairs={{0,96},{16,112},{32,0},{48,16},{64,32},{80,48},{96,64},{112,80},{1... | collective-permute-start | bytes 135176 | tf_op jit(solution)/shard_map/ppermute | solution.py:338
